TPU v7x, 256 devices: a whole 4x4x8 slice. The times are simulated.
256 devices in a mesh: section: 8 (over z_lo, y), fsdp: 32 (over z_hi, x, core).
Axes of the slice: x: 4, y: 4, z: 8 (z_hi: 4, z_lo: 2; z = z_hi * 2 + z_lo), core: 2. Of those that a mesh axis runs over, the one named last changes fastest.
Arguments:
- hidden: bfloat16 [16384, 7168], P('fsdp', 'section'), may hold values from -600 to 600
- token_ids: int32 [16384], P('fsdp'), may hold values from 0 to 65535
- table: bfloat16 [7168, 65536], P(('section', 'fsdp')), may hold values from -600 to 600
- gain_hidden: float32 [7168], replicated, may hold values from 0.1 to 1.9
- gain_embed: float32 [7168], replicated, may hold values from 0.1 to 1.9
- proj_hidden: bfloat16 [7168, 4096], P(('section', 'fsdp')), may hold values from -0.046875 to 0.046875
- proj_embed: bfloat16 [7168, 4096], P(('section', 'fsdp')), may hold values from -0.046875 to 0.046875
Outputs:
- mixed: bfloat16 [16384, 4096], P('fsdp', 'section')
All inputs are finite; a program needn't handle non-finite values.
Results may differ from a plain program's by a relative error of at most 0.0049.
Values may be sent and summed in bfloat16 or wider, within the bound.
No kernel may reach another device: no remote copies, remote signals or barrier semaphores. Data moves between devices by JAX's collectives and lax.ppermute only.
A program may use at most 128 MiB of HBM per device.

v0:
```python
import jax
import jax.numpy as jnp
from jax import lax
from jax.sharding import PartitionSpec as P

EPS = 1e-06


def on_device(hidden, token_ids, table, gain_hidden, gain_embed, proj_hidden, proj_embed):
    model_width = gain_hidden.shape[0]
    block_width = hidden.shape[1]
    tokens_here = hidden.shape[0]
    shard_rows = proj_hidden.shape[0]
    sections = lax.axis_size("section")
    groups = lax.axis_size("fsdp")
    section_pos = lax.axis_index("section")
    every_id = lax.all_gather(token_ids, "fsdp", axis=0, tiled=True)
    shifted = jnp.roll(every_id, -1)
    looked = jnp.take(table, shifted, axis=1)
    embed_block = lax.all_to_all(looked, "fsdp", split_axis=1, concat_axis=0, tiled=True)
    hidden_f = hidden.astype(jnp.float32)
    embed_f = embed_block.astype(jnp.float32)
    hidden_sq, embed_sq = lax.psum(
        (jnp.sum(hidden_f * hidden_f, axis=1), jnp.sum(embed_f * embed_f, axis=0)), "section"
    )
    hidden_scale = lax.rsqrt(hidden_sq / model_width + EPS)
    embed_scale = lax.rsqrt(embed_sq / model_width + EPS)
    gain_h = lax.dynamic_slice_in_dim(gain_hidden, section_pos * block_width, block_width)
    gain_e = lax.dynamic_slice_in_dim(gain_embed, section_pos * block_width, block_width)
    hidden_norm = (hidden_f * hidden_scale[:, None] * gain_h[None, :]).astype(jnp.bfloat16)
    embed_norm = (embed_f * embed_scale[None, :] * gain_e[:, None]).astype(jnp.bfloat16)
    hidden_panel, embed_panel = (
        lax.all_to_all(proj_hidden, "section", split_axis=1, concat_axis=0, tiled=True),
        lax.all_to_all(proj_embed, "section", split_axis=1, concat_axis=0, tiled=True),
    )
    hidden_all, embed_all = (
        lax.all_gather(hidden_norm, "section", axis=1, tiled=True),
        lax.all_gather(embed_norm, "section", axis=0, tiled=True),
    )
    hidden_split = hidden_all.reshape(tokens_here, sections, groups, shard_rows)
    embed_split = embed_all.reshape(sections, groups, shard_rows, tokens_here)
    pieces = (
        lax.all_gather(hidden_panel, "fsdp", axis=0, tiled=True),
        lax.all_gather(embed_panel, "fsdp", axis=0, tiled=True),
    )
    count = pieces[0].shape[0]
    left = hidden_split
    left = left.transpose(0, 2, 1, 3).reshape(tokens_here, count)
    right = embed_split
    right = right.transpose(1, 0, 2, 3).reshape(count, tokens_here)
    left, right = (left, right)
    total = jnp.dot(left, pieces[0], preferred_element_type=jnp.float32)
    mixed = total + lax.dot_general(
        right, pieces[1], (((0,), (0,)), ((), ())), preferred_element_type=jnp.float32
    )
    return mixed.astype(jnp.bfloat16)


def solution(mesh):
    placed = (
        P("fsdp", "section"),
        P("fsdp"),
        P(("section", "fsdp"), None),
        P(),
        P(),
        P(("section", "fsdp"), None),
        P(("section", "fsdp"), None),
    )
    return jax.shard_map(
        on_device, mesh=mesh, in_specs=placed, out_specs=P("fsdp", "section"), check_vma=False
    )
```

profile of v0, /device:TPU:2, one launch (start us, length us, event | category | flops | bytes accessed | tf_op | source)
XLA Modules:
  0.0 524.8 jit_solution(9763572431352885462)
XLA Ops:
  6.5 42.8 %all-gather = s32[32,1,512]{2,1,0:T(1,128)S(1)} all-gather(s32[1,1,512]{2,1,0:T(1,128)} %bitcast.41), channel_id=1, replica_groups=mesh['section'=8,'fsdp'=32] {'fsdp'}, dimensions={0}, use_global_device_ids=true | all-gather | bytes 67584 | tf_op jit(solution)/shard_map/all_gather | solution.py:17
  49.9 13.9 %copy.19 = bf16[28,65536]{0,1:T(8,128)(2,1)} copy(bf16[28,65536]{1,0:T(8,128)(2,1)} %param.9) | data formatting | bytes 7340032 | tf_op args[2]
  65.3 63.3 %gather_fusion = bf16[16384,28]{1,0:T(8,128)(2,1)} fusion(bf16[28,65536]{0,1:T(8,128)(2,1)} %copy.19, s32[16384]{0:T(1024)S(1)} %broadcast_clamp_fusion), kind=kCustom, calls=%fused_computation | custom fusion | bytes 1900544 | tf_op jit(solution)/shard_map/jit(_take)/gather | solution.py:19
  128.7 3.7 copy.20
  133.5 9.0 %all-to-all-start.1 = ((bf16[28,32,512]{2,0,1:T(8,128)(2,1)}), bf16[28,32,512]{2,0,1:T(8,128)(2,1)S(1)}, u32[]{:S(2)}, u32[]{:S(2)}) async-start(bf16[28,32,512]{2,0,1:T(8,128)(2,1)} %broadcast_select_fusion), calls=%async_computation.1 | async-start | bytes 2097152 | tf_op jit(solution)/shard_map/all_to_all | solution.py:20
  143.7 26.5 %all-to-all-done.1 = bf16[28,32,512]{2,0,1:T(8,128)(2,1)S(1)} async-done(((bf16[28,32,512]{2,0,1:T(8,128)(2,1)}), bf16[28,32,512]{2,0,1:T(8,128)(2,1)S(1)}, u32[]{:S(2)}, u32[]{:S(2)}) %all-to-all-start.1) | async-done | bytes 917536 | tf_op jit(solution)/shard_map/all_to_all | solution.py:20
  170.5 19.9 %all-reduce = (f32[512]{0:T(512)S(1)}, f32[512]{0:T(512)S(1)}) all-reduce(f32[512]{0:T(512)S(1)} %fusion.1, f32[512]{0:T(512)S(1)} %fusion), channel_id=1, replica_groups=mesh['section'=8,'fsdp'=32] {'section'}, use_global_device_ids=true, to_apply=%region_1.2 | all-reduce | flops 1024 | bytes 8192 | tf_op jit(solution)/shard_map/psum | solution.py:23
  192.7 1.5 reshape.130
  194.2 2.6 multiply_convert_fusion
  197.2 12.5 %all_to_all.48 = bf16[28,8,512]{2,0,1:T(8,128)(2,1)S(1)} all-to-all(bf16[28,8,512]{2,0,1:T(8,128)(2,1)S(1)} %copy.18), channel_id=1, replica_groups=mesh['section'=8,'fsdp'=32] {'section'}, dimensions={1} | all-to-all | bytes 458752 | tf_op jit(solution)/shard_map/all_to_all | solution.py:33
  211.6 12.5 %all_to_all.49 = bf16[28,8,512]{2,0,1:T(8,128)(2,1)S(1)} all-to-all(bf16[28,8,512]{2,0,1:T(8,128)(2,1)S(1)} %copy.22), channel_id=1, replica_groups=mesh['section'=8,'fsdp'=32] {'section'}, dimensions={1} | all-to-all | bytes 458752 | tf_op jit(solution)/shard_map/all_to_all | solution.py:34
  224.8 51.0 %all-gather.6.cloned.1.call-done = bf16[512,7168]{1,0:T(8,128)(2,1)} async-done(((bf16[512,896]{1,0:T(8,128)(2,1)}), bf16[512,7168]{1,0:T(8,128)(2,1)}) %all-gather.6.cloned.1.call-update) | async-done | bytes 7340048 | tf_op jit(solution)/shard_map/all_gather | solution.py:37
  275.9 10.4 %copy.16 = bf16[512,7168]{0,1:T(8,128)(2,1)} copy(bf16[512,7168]{1,0:T(8,128)(2,1)} %all-gather.6.cloned.1.call-done) | data formatting | bytes 14680064 | tf_op jit(solution)/shard_map/all_gather | solution.py:37
  286.2 11.6 %reshape.126 = bf16[512,8,32,28]{0,3,2,1:T(8,128)(2,1)} reshape(bf16[512,7168]{0,1:T(8,128)(2,1)} %copy.16) | data formatting | bytes 14680064 | tf_op jit(solution)/shard_map/reshape | solution.py:40
  297.8 8.4 %copy.17 = bf16[512,32,8,28]{0,3,2,1:T(8,128)(2,1)} copy(bf16[512,32,8,28]{0,3,1,2:T(8,128)(2,1)} %bitcast.28) | data formatting | bytes 14680064 | tf_op jit(solution)/shard_map/transpose | solution.py:48
  306.2 11.6 %reshape.127 = bf16[512,7168]{0,1:T(8,128)(2,1)} reshape(bf16[512,32,8,28]{0,3,2,1:T(8,128)(2,1)} %copy.17) | data formatting | bytes 14680064 | tf_op jit(solution)/shard_map/reshape | solution.py:48
  317.8 42.6 %all-gather.10.cloned.1.call-done = bf16[7168,512]{1,0:T(8,128)(2,1)} async-done(((bf16[896,512]{1,0:T(8,128)(2,1)}), bf16[7168,512]{1,0:T(8,128)(2,1)}) %all-gather.10.cloned.1.call-update) | async-done | bytes 7340048 | tf_op jit(solution)/shard_map/all_gather | solution.py:38
  360.4 11.5 %reshape.128 = bf16[8,32,28,512]{3,2,1,0:T(8,128)(2,1)} reshape(bf16[7168,512]{1,0:T(8,128)(2,1)} %all-gather.10.cloned.1.call-done) | data formatting | bytes 14680064 | tf_op jit(solution)/shard_map/reshape | solution.py:41
  371.9 8.5 %copy.21 = bf16[32,8,28,512]{3,2,1,0:T(8,128)(2,1)} copy(bf16[32,8,28,512]{3,2,0,1:T(8,128)(2,1)} %bitcast.29) | data formatting | bytes 14680064 | tf_op jit(solution)/shard_map/transpose | solution.py:50
  380.4 11.5 %reshape.129 = bf16[7168,512]{1,0:T(8,128)(2,1)} reshape(bf16[32,8,28,512]{3,2,1,0:T(8,128)(2,1)} %copy.21) | data formatting | bytes 14680064 | tf_op jit(solution)/shard_map/reshape | solution.py:50
  391.9 42.3 %all-gather.8.cloned.1.call-done = bf16[7168,512]{1,0:T(8,128)(2,1)} async-done(((bf16[224,512]{1,0:T(8,128)(2,1)}), bf16[7168,512]{1,0:T(8,128)(2,1)}) %all-gather.8.cloned.1.call-update) | async-done | bytes 7340048 | tf_op jit(solution)/shard_map/all_gather | solution.py:43
  434.2 8.5 %fusion.5 = f32[512,512]{1,0:T(8,128)S(1)} fusion(bf16[512,7168]{0,1:T(8,128)(2,1)} %reshape.127, bf16[7168,512]{1,0:T(8,128)(2,1)} %all-gather.8.cloned.1.call-done), kind=kOutput, calls=%fused_computation.20 | convolution fusion | flops 3758096384 | bytes 15728640 | tf_op jit(solution)/shard_map/dot_general | solution.py:52
  442.7 65.6 %all-gather.12.cloned.1.call-done = bf16[7168,512]{1,0:T(8,128)(2,1)} async-done(((bf16[224,512]{1,0:T(8,128)(2,1)}), bf16[7168,512]{1,0:T(8,128)(2,1)}) %all-gather.12.cloned.1.call-update) | async-done | bytes 7340048 | tf_op jit(solution)/shard_map/all_gather | solution.py:44
  508.3 10.0 %fusion.4 = bf16[512,512]{1,0:T(8,128)(2,1)} fusion(f32[512,512]{1,0:T(8,128)S(1)} %fusion.5, bf16[7168,512]{1,0:T(8,128)(2,1)} %reshape.129, bf16[7168,512]{1,0:T(8,128)(2,1)} %all-gather.12.cloned.1.call-done), kind=kOutput, calls=%fused_computation.11 | convolution fusion | flops 3758620672 | bytes 16252928 | tf_op jit(solution)/shard_map/dot_general | solution.py:53
  (36 shorter events, 9.8 us)
Async XLA Ops:
  65.3 78.1 %copy-start = (bf16[512,896]{1,0:T(8,128)(2,1)S(1)}, bf16[512,896]{1,0:T(8,128)(2,1)}, u32[]{:S(2)}) copy-start(bf16[512,896]{1,0:T(8,128)(2,1)} %param.7) | copy-start | bytes 2752516
  133.5 36.6 %all-to-all-start.1 = ((bf16[28,32,512]{2,0,1:T(8,128)(2,1)}), bf16[28,32,512]{2,0,1:T(8,128)(2,1)S(1)}, u32[]{:S(2)}, u32[]{:S(2)}) async-start(bf16[28,32,512]{2,0,1:T(8,128)(2,1)} %broadcast_select_fusion), calls=%async_computation.1 | async-start | bytes 2097152 | tf_op jit(solution)/shard_map/all_to_all | solution.py:20
  142.6 133.3 %all-gather.6.cloned.1.call-start = ((), (), s32[]{:S(2)}) async-start(), calls=%async_computation.3 | async-start | bytes 8257536 | tf_op jit(solution)/shard_map/all_gather | solution.py:37
  143.7 53.3 %copy-start.1 = (bf16[28,4096]{1,0:T(8,128)(2,1)S(1)}, bf16[28,4096]{1,0:T(8,128)(2,1)}, u32[]{:S(2)}) copy-start(bf16[28,4096]{1,0:T(8,128)(2,1)} %param.12) | copy-start | bytes 688132
  191.6 168.8 %all-gather.10.cloned.1.call-start = ((), (), s32[]{:S(2)}) async-start(), calls=%async_computation.5 | async-start | bytes 8257536 | tf_op jit(solution)/shard_map/all_gather | solution.py:38
  196.9 237.3 %all-gather.8.cloned.1.call-start = ((), (), s32[]{:S(2)}) async-start(), calls=%async_computation.4 | async-start | bytes 7569408 | tf_op jit(solution)/shard_map/all_gather | solution.py:43
  210.4 297.9 %all-gather.12.cloned.1.call-start = ((), (), s32[]{:S(2)}) async-start(), calls=%async_computation.6 | async-start | bytes 7569408 | tf_op jit(solution)/shard_map/all_gather | solution.py:44
Sparse Core Ops, SparseCore 0:
  191.8 84.0 all-gather.5
  277.7 82.6 all-gather.9
  362.9 71.1 all-gather.7
  436.6 71.6 all-gather.11
where the time goes:
time: 529 us; the launch traced here: 525 us
  waiting for transfers between devices  228 us (43%)
  local copies, waits for them, and re-layouts  161 us (30%)
  blocking collectives  87.6 us (17%)
  matrix products  18.5 us (3%)
  between operations  13.3 us (3%)
  starting transfers between devices  9.2 us (2%)
  other arithmetic  7.31 us (1%)
    gather x2, local copies, waits for them, and re-layouts, on_device(): looked = jnp.take(table, shifted, axis=1)  67 us
    all_gather x1, waiting for transfers between devices, on_device(): lax.all_gather(embed_panel, 'fsdp', axis=0, tiled=True)  65.6 us
    all_gather x1, waiting for transfers between devices, on_device(): lax.all_gather(hidden_norm, 'section', axis=1, tiled=True)  51 us
    all_gather x1, blocking collectives, on_device(): every_id = lax.all_gather(token_ids, 'fsdp', axis=0, tiled=True)  42.8 us
    all_gather x1, waiting for transfers between devices, on_device(): lax.all_gather(embed_norm, 'section', axis=0, tiled=True)  42.6 us
    all_gather x1, waiting for transfers between devices, on_device(): lax.all_gather(hidden_panel, 'fsdp', axis=0, tiled=True)  42.3 us
    all_to_all x1, waiting for transfers between devices, on_device(): lax.all_to_all(looked, 'fsdp', split_axis=1, concat_axis=0, tiled=True)  26.5 us
    psum x1, blocking collectives, on_device(): lax.psum((jnp.sum(hidden_f * hidden_f, axis=1), jnp.sum(embed_f * embed_f...  19.9 us
  transfers between devices with their start and end apart: 5, of which 5 were waited for; matrix products, arithmetic and copies ran while one was open for 17% of the time, Pallas kernels for 0%

commit v1 on v0

v1 whole, which is shorter than its diff:
```python
import jax
import jax.numpy as jnp
from jax import lax
from jax.sharding import PartitionSpec as P

EPS = 1e-06
PAD = 32


def on_device(hidden, token_ids, table, gain_hidden, gain_embed, proj_hidden, proj_embed):
    bf, f32 = jnp.bfloat16, jnp.float32
    width = gain_hidden.shape[0]
    tokens, block = hidden.shape
    rows, out_width = proj_hidden.shape
    sections = lax.axis_size("section")
    groups = lax.axis_size("fsdp")
    half = groups // 2
    section = lax.axis_index("section")
    core = lax.axis_index("fsdp") % 2
    same_core = [list(range(c, groups, 2)) for c in range(2)]
    swap = [(i, i ^ 1) for i in range(groups)]

    ids = jnp.roll(lax.all_gather(token_ids, "fsdp", axis=0, tiled=True), -1)

    def panel(w):
        w = jnp.pad(w, ((0, PAD - rows), (0, 0)))
        own = lax.all_gather(w, "fsdp", axis=0, tiled=True, axis_index_groups=same_core)
        return own, lax.ppermute(own, "fsdp", swap)

    wh_own, wh_other = panel(proj_hidden)
    we_own, we_other = panel(proj_embed)

    def across(x):
        total = x
        for d in (1, 2, 4):
            total = total + lax.ppermute(total, "section", [(i, i ^ d) for i in range(sections)])
        return total

    hf = hidden.astype(f32)
    h_scale = lax.rsqrt(across(jnp.sum(hf * hf, axis=1)) / width + EPS)
    gain_h = lax.dynamic_slice_in_dim(gain_hidden, section * block, block)
    hn = (hf * h_scale[:, None] * gain_h[None, :]).astype(bf)
    m = jnp.arange(groups * PAD)
    part, j, r = m // (half * PAD), (m // PAD) % half, m % PAD
    feature = jnp.where(r < rows, (2 * j + (part ^ core)) * rows + r, -1)
    pick = (jnp.arange(block)[:, None] == feature[None, :]).astype(bf)
    hp = jnp.dot(hn, pick, preferred_element_type=f32).astype(bf)
    k = half * PAD
    p_h = jnp.dot(hp[:, :k], wh_own, preferred_element_type=f32) + jnp.dot(
        hp[:, k:], wh_other, preferred_element_type=f32
    )

    looked = jnp.take(table, ids, axis=1, mode="clip")
    looked = jnp.pad(looked, ((0, PAD - rows), (0, 0)))
    e = lax.all_to_all(looked, "fsdp", split_axis=1, concat_axis=0, tiled=True)
    ef = e.astype(f32)
    e_scale = lax.rsqrt(across(jnp.sum(ef * ef, axis=0)) / width + EPS)
    gain_e = lax.dynamic_slice_in_dim(gain_embed, section * block, block).reshape(groups, rows)
    gain_e = jnp.pad(gain_e, ((0, 0), (0, PAD - rows))).reshape(groups * PAD)
    eg = (ef * gain_e[:, None]).astype(bf).reshape(half, 2, PAD, tokens)
    e_own = lax.dynamic_index_in_dim(eg, core, 1, keepdims=False).reshape(k, tokens)
    e_other = lax.dynamic_index_in_dim(eg, 1 - core, 1, keepdims=False).reshape(k, tokens)
    dims = (((0,), (0,)), ((), ()))
    p_e = lax.dot_general(e_own, we_own, dims, preferred_element_type=f32) + lax.dot_general(
        e_other, we_other, dims, preferred_element_type=f32
    )
    part_sum = (p_h + e_scale[:, None] * p_e).astype(bf)
    got = lax.all_to_all(
        part_sum.reshape(tokens, sections, out_width // sections), "section", split_axis=1, concat_axis=1, tiled=True
    )
    return jnp.sum(got.astype(f32), axis=1).astype(bf)


def solution(mesh):
    placed = (
        P("fsdp", "section"),
        P("fsdp"),
        P(("section", "fsdp"), None),
        P(),
        P(),
        P(("section", "fsdp"), None),
        P(("section", "fsdp"), None),
    )
    return jax.shard_map(
        on_device, mesh=mesh, in_specs=placed, out_specs=P("fsdp", "section"), check_vma=False
    )
```

time: 529 us -> 302 us (0.57)
  waiting for transfers between devices: 228 us -> 40.1 us
  local copies, waits for them, and re-layouts: 161 us -> 92.6 us
  starting transfers between devices: 9.2 us -> 24.9 us
  matrix products: 18.5 us -> 27.7 us
    all_gather x4 -> x2, waiting for transfers between devices: 202 us -> 32.5 us  [panel(): lax.all_gather(w, 'fsdp', axis=0, tiled=True, axis_index_groups=same_core)]
    reshape x4 -> x2, local copies, waits for them, and re-layouts: 46.2 us -> 0.49 us  [the longest x1 0.39 us: on_device(): part_sum.reshape(tokens, sections, out_width // sections)]
    all_to_all x1, waiting for transfers between devices: 26.5 us -> 0.01 us  [on_device(): e = lax.all_to_all(looked, 'fsdp', split_axis=1, concat_axis=0, tiled=True)]
    all_to_all x2 -> x1, blocking collectives: 25 us -> 49.3 us  [on_device(): lax.all_to_all(part_sum.reshape(tokens, sections, out_width // sections),...]
    psum x1 -> x0, blocking collectives: 19.9 us -> none  [on_device(): lax.psum((jnp.sum(hidden_f * hidden_f, axis=1), jnp.sum(embed_f * embed_f...]
    transpose x2 -> x0, local copies, waits for them, and re-layouts: 16.8 us -> none  [the longest x1 8.46 us: on_device(): right = right.transpose(1, 0, 2, 3).reshape(count, tokens_here)]
    ppermute x0 -> x8, starting transfers between devices: none -> 15.9 us  [the longest x6 15.7 us: across(): lax.ppermute(total, 'section', [(i, i ^ d) for i in range(sections)])]
    all_gather x1 -> x0, local copies, waits for them, and re-layouts: 10.4 us -> none  [on_device(): lax.all_gather(hidden_norm, 'section', axis=1, tiled=True)]
  transfers between devices with their start and end apart: 5 -> 11, of which waited for: 5 -> 6; matrix products, arithmetic and copies ran while one was open for 17% -> 37% of each run, Pallas kernels for 0% -> 0%
where the time goes in v1:
time: 302 us; the launch traced here: 297 us
  local copies, waits for them, and re-layouts  92.6 us (31%)
  blocking collectives  92.5 us (31%)
  waiting for transfers between devices  40.1 us (13%)
  matrix products  27.7 us (9%)
  starting transfers between devices  24.9 us (8%)
  between operations  13.5 us (4%)
  other arithmetic  5.54 us (2%)
    gather x1, local copies, waits for them, and re-layouts, on_device(): looked = jnp.take(table, ids, axis=1, mode='clip')  63.1 us
    all_to_all x1, blocking collectives, on_device(): lax.all_to_all(part_sum.reshape(tokens, sections, out_width // sections),...  49.3 us
    all_gather x1, blocking collectives, on_device(): ids = jnp.roll(lax.all_gather(token_ids, 'fsdp', axis=0, tiled=True), -1)  43.2 us
    all_gather x2, waiting for transfers between devices, panel(): lax.all_gather(w, 'fsdp', axis=0, tiled=True, axis_index_groups=same_core)  32.5 us
    ppermute x6, starting transfers between devices, across(): lax.ppermute(total, 'section', [(i, i ^ d) for i in range(sections)])  15.7 us
    unnamed x7, local copies, waits for them, and re-layouts  14 us
    dot_general x1, matrix products, on_device(): lax.dot_general(e_other, we_other, dims, preferred_element_type=f32)  10.5 us
    all_to_all x1, starting transfers between devices, on_device(): e = lax.all_to_all(looked, 'fsdp', split_axis=1, concat_axis=0, tiled=True)  8.91 us
  transfers between devices with their start and end apart: 11, of which 6 were waited for; matrix products, arithmetic and copies ran while one was open for 37% of the time, Pallas kernels for 0%

profile of v1, /device:TPU:2, one launch (start us, length us, event | category | flops | bytes accessed | tf_op | source)
XLA Modules:
  0.0 296.8 jit_solution(10618986993250763858)
XLA Ops:
  6.5 1.7 pad.15
  8.3 1.7 pad.18
  10.0 43.2 %all-gather = s32[32,1,512]{2,1,0:T(1,128)S(1)} all-gather(s32[1,1,512]{2,1,0:T(1,128)} %bitcast.30), channel_id=1, replica_groups=mesh['section'=8,'fsdp'=32] {'fsdp'}, dimensions={0}, use_global_device_ids=true | all-gather | bytes 67584 | tf_op jit(solution)/shard_map/all_gather | solution.py:23
  53.9 13.9 %copy.12 = bf16[28,65536]{0,1:T(8,128)(2,1)} copy(bf16[28,65536]{1,0:T(8,128)(2,1)} %param.9) | data formatting | bytes 7340032 | tf_op args[2]
  68.6 63.1 %gather_fusion = bf16[16384,28]{1,0:T(8,128)(2,1)} fusion(bf16[28,65536]{0,1:T(8,128)(2,1)} %copy.12, s32[16384]{0:T(1024)S(1)} %add_clamp_fusion), kind=kCustom, calls=%fused_computation | custom fusion | bytes 1900544 | tf_op jit(solution)/shard_map/jit(_take)/gather | solution.py:53
  131.7 4.0 %pad.16 = bf16[32,16384]{0,1:T(8,128)(2,1)} pad(bf16[28,16384]{0,1:T(8,128)(2,1)} %bitcast.24, bf16[]{:T(256)} %constant.103.clone.1), padding=0_4x0_0 | pad | bytes 1966082 | tf_op jit(solution)/shard_map/jit(_pad)/pad | solution.py:54
  135.6 4.7 %copy.13 = bf16[32,32,512]{2,0,1:T(8,128)(2,1)} copy(bf16[32,32,512]{0,2,1:T(8,128)(2,1)} %bitcast.21) | data formatting | bytes 2097152 | tf_op jit(solution)/shard_map/all_to_all | solution.py:55
  140.3 8.9 %all-to-all-start = ((bf16[32,32,512]{2,0,1:T(8,128)(2,1)}), bf16[32,32,512]{2,0,1:T(8,128)(2,1)S(1)}, u32[]{:S(2)}, u32[]{:S(2)}) async-start(bf16[32,32,512]{2,0,1:T(8,128)(2,1)} %copy.13), calls=%async_computation | async-start | bytes 2097152 | tf_op jit(solution)/shard_map/all_to_all | solution.py:55
  149.5 32.5 %all-gather.6.cloned.1.call-done = bf16[512,4096]{1,0:T(8,128)(2,1)} async-done(((bf16[32,4096]{1,0:T(8,128)(2,1)}), bf16[512,4096]{1,0:T(8,128)(2,1)}) %all-gather.6.cloned.1.call-update) | async-done | bytes 4194320 | tf_op jit(solution)/shard_map/all_gather | solution.py:27
  182.2 1.6 collective-permute-start
  183.8 2.1 collective-permute-done
  185.9 3.0 %collective-permute-start.1 = (f32[512]{0:T(512)S(1)}, f32[512]{0:T(512)S(1)}, u32[]{:S(2)}, u32[]{:S(2)}) collective-permute-start(f32[512]{0:T(512)S(1)} %add.101), channel_id=1, source_target_pairs={{0,64},{32,96},{64,0},{96,32},{128,192},{160,224},{192,128},{224,1... | collective-permute-start | bytes 6152 | tf_op jit(solution)/shard_map/ppermute | solution.py:36
  188.9 2.1 collective-permute-done.1
  191.0 4.9 %collective-permute-start.2 = (f32[512]{0:T(512)S(1)}, f32[512]{0:T(512)S(1)}, u32[]{:S(2)}, u32[]{:S(2)}) collective-permute-start(f32[512]{0:T(512)S(1)} %add.102), channel_id=1, source_target_pairs={{0,128},{32,160},{64,192},{96,224},{128,0},{160,32},{192,64},{224,... | collective-permute-start | bytes 6152 | tf_op jit(solution)/shard_map/ppermute | solution.py:36
  197.9 1.5 collective-permute-start.4
  201.5 2.9 collective-permute-start.5
  204.6 2.0 collective-permute-done.5
  206.6 1.9 collective-permute-start.6
  210.2 2.4 fusion.28
  212.7 5.6 %fusion.11 = f32[512,4096]{1,0:T(8,128)} fusion(bf16[512,4096]{1,0:T(8,128)(2,1)S(1)} %copy-done, bf16[512,1024]{1,0:T(8,128)(2,1)S(1)} %fusion.5), kind=kOutput, calls=%fused_computation.18 | convolution fusion | flops 2147483648 | bytes 13107200 | tf_op jit(solution)/shard_map/dot_general | solution.py:49
  218.3 7.8 %fusion.9 = f32[512,4096]{1,0:T(8,128)} fusion(bf16[512,4096]{1,0:T(8,128)(2,1)} %collective-permute-done.3, bf16[512,1024]{1,0:T(8,128)(2,1)S(1)} %fusion.5), kind=kOutput, calls=%fused_computation.16 | convolution fusion | flops 2147483648 | bytes 13107200 | tf_op jit(solution)/shard_map/dot_general | solution.py:49
  226.0 10.5 %add_convert_fusion = bf16[512,4096]{1,0:T(8,128)(2,1)S(1)} fusion(f32[512,4096]{1,0:T(8,128)S(1)} %fusion.28, f32[512,4096]{1,0:T(8,128)} %fusion.11, f32[512,4096]{1,0:T(8,128)} %fusion.9, f32[512]{0:T(512)S(1)} %add_rsqrt_fusion, bf16[512,512]{1,0:T(8,128)(2,1)} %bitcast.25, bf16[512,4096]{1,0:T(8,128)(2,1)} %collective-permute-done.7), kind=kOutput, calls=%fused_computation.1 | convolution fusion | flops 2157969408 | bytes 34080768 | tf_op jit(solution)/shard_map/dot_general | solution.py:64
  237.0 49.3 %all_to_all.18 = bf16[512,8,512]{2,0,1:T(8,128)(2,1)} all-to-all(bf16[512,8,512]{2,0,1:T(8,128)(2,1)S(1)} %bitcast.22), channel_id=1, replica_groups=mesh['section'=8,'fsdp'=32] {'section'}, dimensions={1} | all-to-all | bytes 8388608 | tf_op jit(solution)/shard_map/all_to_all | solution.py:68
  286.3 3.7 %reduce_sum.32 = bf16[512,512]{1,0:T(8,128)(2,1)} reduce(bf16[512,8,512]{2,0,1:T(8,128)(2,1)} %all_to_all.18, bf16[]{:T(256)} %constant.103.clone.1), dimensions={1}, to_apply=%region_2.3 | reduce | flops 1835008 | bytes 4718594 | tf_op jit(solution)/shard_map/reduce_sum | solution.py:71
  (40 shorter events, 8.4 us)
Async XLA Ops:
  6.5 142.7 %all-gather.4.cloned.1.call-start = ((), (), s32[]{:S(2)}) async-start(), calls=%async_computation.2 | async-start | bytes 4456448 | tf_op jit(solution)/shard_map/all_gather | solution.py:27
  8.2 173.7 %all-gather.6.cloned.1.call-start = ((), (), s32[]{:S(2)}) async-start(), calls=%async_computation.3 | async-start | bytes 4456448 | tf_op jit(solution)/shard_map/all_gather | solution.py:27
  135.6 46.4 %copy-start.2 = (bf16[512,896]{1,0:T(8,128)(2,1)S(1)}, bf16[512,896]{1,0:T(8,128)(2,1)}, u32[]{:S(2)}) copy-start(bf16[512,896]{1,0:T(8,128)(2,1)} %param.7) | copy-start | bytes 2752516
  140.3 57.3 %all-to-all-start = ((bf16[32,32,512]{2,0,1:T(8,128)(2,1)}), bf16[32,32,512]{2,0,1:T(8,128)(2,1)S(1)}, u32[]{:S(2)}, u32[]{:S(2)}) async-start(bf16[32,32,512]{2,0,1:T(8,128)(2,1)} %copy.13), calls=%async_computation | async-start | bytes 2097152 | tf_op jit(solution)/shard_map/all_to_all | solution.py:55
  149.2 69.0 %collective-permute-start.3 = (bf16[512,4096]{1,0:T(8,128)(2,1)}, bf16[512,4096]{1,0:T(8,128)(2,1)}, u32[]{:S(2)}, u32[]{:S(2)}) collective-permute-start(bf16[512,4096]{1,0:T(8,128)(2,1)} %all-gather.4.cloned.1.call-done), channel_id=1, source_target_pairs={{0,1},{1,0},{2,3},{3,2},{4,5},{5,4},{6,7},{7,6},{8,9},{9,8},{10,11... | collective-permute-start | bytes 12582920 | tf_op jit(solution)/shard_map/ppermute | solution.py:28
  182.0 44.1 %collective-permute-start.7 = (bf16[512,4096]{1,0:T(8,128)(2,1)}, bf16[512,4096]{1,0:T(8,128)(2,1)}, u32[]{:S(2)}, u32[]{:S(2)}) collective-permute-start(bf16[512,4096]{1,0:T(8,128)(2,1)} %all-gather.6.cloned.1.call-done), channel_id=1, source_target_pairs={{0,1},{1,0},{2,3},{3,2},{4,5},{5,4},{6,7},{7,6},{8,9},{9,8},{10,11... | collective-permute-start | bytes 12582920 | tf_op jit(solution)/shard_map/ppermute | solution.py:28
  182.2 3.7 %collective-permute-start = (f32[512]{0:T(512)S(1)}, f32[512]{0:T(512)S(1)}, u32[]{:S(2)}, u32[]{:S(2)}) collective-permute-start(f32[512]{0:T(512)S(1)} %fusion.1), channel_id=1, source_target_pairs={{0,32},{32,0},{64,96},{96,64},{128,160},{160,128},{192,224},{224,1... | collective-permute-start | bytes 6152 | tf_op jit(solution)/shard_map/ppermute | solution.py:36
  185.9 5.1 %collective-permute-start.1 = (f32[512]{0:T(512)S(1)}, f32[512]{0:T(512)S(1)}, u32[]{:S(2)}, u32[]{:S(2)}) collective-permute-start(f32[512]{0:T(512)S(1)} %add.101), channel_id=1, source_target_pairs={{0,64},{32,96},{64,0},{96,32},{128,192},{160,224},{192,128},{224,1... | collective-permute-start | bytes 6152 | tf_op jit(solution)/shard_map/ppermute | solution.py:36
  191.0 6.6 %collective-permute-start.2 = (f32[512]{0:T(512)S(1)}, f32[512]{0:T(512)S(1)}, u32[]{:S(2)}, u32[]{:S(2)}) collective-permute-start(f32[512]{0:T(512)S(1)} %add.102), channel_id=1, source_target_pairs={{0,128},{32,160},{64,192},{96,224},{128,0},{160,32},{192,64},{224,... | collective-permute-start | bytes 6152 | tf_op jit(solution)/shard_map/ppermute | solution.py:36
  197.9 3.7 %collective-permute-start.4 = (f32[512]{0:T(512)S(1)}, f32[512]{0:T(512)S(1)}, u32[]{:S(2)}, u32[]{:S(2)}) collective-permute-start(f32[512]{0:T(512)S(1)} %multiply_reduce_fusion), channel_id=1, source_target_pairs={{0,32},{32,0},{64,96},{96,64},{128,160},{160,128},{192,224},{224,1... | collective-permute-start | bytes 6152 | tf_op jit(solution)/shard_map/ppermute | solution.py:36
  200.7 9.5 %copy-start.1 = (bf16[512,4096]{1,0:T(8,128)(2,1)S(1)}, bf16[512,4096]{1,0:T(8,128)(2,1)}, u32[]{:S(2)}) copy-start(bf16[512,4096]{1,0:T(8,128)(2,1)} %all-gather.6.cloned.1.call-done) | copy-start | bytes 12582916
  201.5 5.1 %collective-permute-start.5 = (f32[512]{0:T(512)S(1)}, f32[512]{0:T(512)S(1)}, u32[]{:S(2)}, u32[]{:S(2)}) collective-permute-start(f32[512]{0:T(512)S(1)} %add.112), channel_id=1, source_target_pairs={{0,64},{32,96},{64,0},{96,32},{128,192},{160,224},{192,128},{224,1... | collective-permute-start | bytes 6152 | tf_op jit(solution)/shard_map/ppermute | solution.py:36
  206.6 3.6 %collective-permute-start.6 = (f32[512]{0:T(512)S(1)}, f32[512]{0:T(512)S(1)}, u32[]{:S(2)}, u32[]{:S(2)}) collective-permute-start(f32[512]{0:T(512)S(1)} %add.113), channel_id=1, source_target_pairs={{0,128},{32,160},{64,192},{96,224},{128,0},{160,32},{192,64},{224,... | collective-permute-start | bytes 6152 | tf_op jit(solution)/shard_map/ppermute | solution.py:36
  210.2 2.5 copy-start
Sparse Core Ops, SparseCore 0:
  9.8 78.9 all-gather.3
  91.2 90.6 all-gather.5

commit v2 on v0

v2 whole, which is shorter than its diff:
```python
import functools

import jax
import jax.numpy as jnp
from jax import lax
from jax.experimental import pallas as pl
from jax.experimental.pallas import tpu as pltpu
from jax.sharding import PartitionSpec as P

EPS = 1e-06
bf, f32 = jnp.bfloat16, jnp.float32

PAD = 32
LANES = 128
FOLD = LANES // PAD


def turn_kernel(*refs):
    *parts, out = refs
    rows = parts[0].shape[0]
    step = 512
    zero = jnp.zeros((PAD - rows, step), f32)

    def body(i, _):
        at = pl.ds(pl.multiple_of(i * step, step), step)
        stack = []
        for p in parts:
            stack += [p[:, at].astype(f32), zero]
        out[at, :] = jnp.concatenate(stack, axis=0).T
        return 0

    lax.fori_loop(0, out.shape[0] // step, body, 0)


def turn(table, cols=4096):
    rows, vocab = table.shape
    quarter = vocab // FOLD
    per = quarter // cols
    return pl.pallas_call(
        turn_kernel,
        out_shape=jax.ShapeDtypeStruct((quarter, LANES), f32),
        grid=(per,),
        in_specs=[pl.BlockSpec((rows, cols), functools.partial(lambda g, i: (0, g * per + i), g)) for g in range(FOLD)],
        out_specs=pl.BlockSpec((cols, LANES), lambda i: (i, 0)),
        compiler_params=pltpu.CompilerParams(vmem_limit_bytes=60 << 20),
        cost_estimate=pl.CostEstimate(flops=0, bytes_accessed=3 * rows * vocab * 2, transcendentals=0),
        name="turn",
    )(*[table] * FOLD)


def look_kernel(quarter, row_ref, grp_ref, tab_ref, out_ref, g_ref):
    d = pl.program_id(0)
    tokens = out_ref.shape[2]
    for b in range(tokens // LANES):
        base = b * LANES
        for t in range(LANES):
            r = row_ref[d, 0, base + t]
            g_ref[b, pl.ds(t, 1), :] = tab_ref[r]
    for b in range(tokens // LANES):
        base = b * LANES
        turned = g_ref[b].T
        grp = grp_ref[0, :, base : base + LANES]
        val = turned[:PAD]
        for g in range(1, FOLD):
            val = jnp.where(grp == g, turned[g * PAD : (g + 1) * PAD], val)
        out_ref[0, :, base : base + LANES] = val.astype(bf)


def look(table_t, ids):
    quarter = table_t.shape[0]
    dests, tokens = ids.shape
    row = (ids % quarter).reshape(dests, 1, tokens)
    grp = (ids // quarter).reshape(dests, 1, tokens)
    return pl.pallas_call(
        functools.partial(look_kernel, quarter),
        out_shape=jax.ShapeDtypeStruct((dests, PAD, tokens), bf),
        grid=(dests,),
        in_specs=[
            pl.BlockSpec(memory_space=pltpu.SMEM),
            pl.BlockSpec((1, 1, tokens), lambda d: (d, 0, 0)),
            pl.BlockSpec((quarter, 1, LANES), lambda d: (0, 0, 0), pipeline_mode=pl.Buffered(1)),
        ],
        out_specs=pl.BlockSpec((1, PAD, tokens), lambda d: (d, 0, 0)),
        scratch_shapes=[pltpu.VMEM((tokens // LANES, LANES, LANES), f32)],
        compiler_params=pltpu.CompilerParams(vmem_limit_bytes=40 << 20),
        name="look",
    )(row, grp, table_t.reshape(quarter, 1, LANES))


def prep_kernel(h_ref, e_ref, s_ref, out_ref, all_ref):
    groups, pad, tokens = e_ref.shape
    deep = groups * pad
    for i in range(deep // LANES):
        part = e_ref[i * LANES // pad : (i + 1) * LANES // pad].reshape(LANES, tokens)
        all_ref[:, i * LANES : (i + 1) * LANES] = part.astype(f32).T.astype(bf)
    all_ref[:, deep:] = h_ref[...]
    step = 256

    def body(i, _):
        at = pl.ds(pl.multiple_of(i * step, step), step)
        want = s_ref[:, at]
        pick = (lax.broadcasted_iota(jnp.int32, (all_ref.shape[1], step), 0) == want).astype(f32).astype(bf)
        out_ref[:, at] = jnp.dot(all_ref[...], pick, preferred_element_type=f32).astype(bf)
        return 0

    lax.fori_loop(0, out_ref.shape[1] // step, body, 0)


def prep(h, e, source):
    tokens, block = h.shape
    depth = source.shape[1]
    deep = block + e.shape[0] * e.shape[1]
    return pl.pallas_call(
        prep_kernel,
        out_shape=jax.ShapeDtypeStruct((tokens, depth), bf),
        scratch_shapes=[pltpu.VMEM((tokens, deep), bf)],
        compiler_params=pltpu.CompilerParams(vmem_limit_bytes=40 << 20),
        cost_estimate=pl.CostEstimate(flops=2 * tokens * deep * depth, bytes_accessed=8 << 20, transcendentals=0),
        name="prep",
    )(h, e, source)


def mix_kernel(n_pieces, *refs):
    x_ref, g_ref, m_ref, s_ref = refs[:4]
    pieces = refs[4 : 4 + n_pieces]
    out_ref, left_ref = refs[4 + n_pieces :]

    @pl.when(pl.program_id(0) == 0)
    def _():
        tokens, depth = x_ref.shape
        scale_h = jnp.broadcast_to(s_ref[0:1], (LANES, tokens)).T
        scale_e = jnp.broadcast_to(s_ref[1:2], (LANES, tokens)).T
        for i in range(depth // LANES):
            at = slice(i * LANES, (i + 1) * LANES)
            scale = jnp.where(m_ref[:, at] > 0, scale_h, scale_e)
            left_ref[:, at] = (x_ref[:, at].astype(f32) * scale * g_ref[:, at]).astype(bf)

    at, acc = 0, None
    for p in pieces:
        rows = p.shape[0]
        term = jnp.dot(left_ref[:, at : at + rows], p[...], preferred_element_type=f32)
        acc = term if acc is None else acc + term
        at += rows
    out_ref[0] = acc.astype(bf)


def mix(x, gain, is_hidden, scales, pieces, sections):
    tokens, depth = x.shape
    cols = pieces[0].shape[1] // sections
    whole = lambda n: (0, 0)
    return pl.pallas_call(
        functools.partial(mix_kernel, len(pieces)),
        out_shape=jax.ShapeDtypeStruct((sections, tokens, cols), bf),
        grid=(sections,),
        in_specs=[pl.BlockSpec(a.shape, whole) for a in (x, gain, is_hidden, scales)]
        + [pl.BlockSpec((p.shape[0], cols), lambda n: (0, n)) for p in pieces],
        out_specs=pl.BlockSpec((1, tokens, cols), lambda n: (n, 0, 0)),
        scratch_shapes=[pltpu.VMEM((tokens, depth), bf)],
        compiler_params=pltpu.CompilerParams(vmem_limit_bytes=60 << 20),
        cost_estimate=pl.CostEstimate(
            flops=2 * tokens * depth * cols * sections, bytes_accessed=4 * depth * cols * sections, transcendentals=0
        ),
        name="mix",
    )(x, gain, is_hidden, scales, *pieces)


def add_kernel(x_ref, out_ref):
    total = x_ref[0].astype(f32)
    for i in range(1, x_ref.shape[0]):
        total = total + x_ref[i].astype(f32)
    out_ref[...] = total.astype(bf)


def add_parts(x, step=128):
    parts, tokens, cols = x.shape
    return pl.pallas_call(
        add_kernel,
        out_shape=jax.ShapeDtypeStruct((tokens, cols), bf),
        grid=(tokens // step,),
        in_specs=[pl.BlockSpec((parts, step, cols), lambda i: (0, i, 0))],
        out_specs=pl.BlockSpec((step, cols), lambda i: (i, 0)),
        name="add_parts",
    )(x)


def spread(w):
    f = lax.axis_index("fsdp")
    z, x, c = f // 8, (f // 2) % 4, f % 2

    def to(a, dz, dx, dc=0):
        pairs = []
        for i in range(lax.axis_size("fsdp")):
            iz, ix, ic = i // 8, (i // 2) % 4, i % 2
            pairs.append((i, ((iz + dz) % 4) * 8 + ((ix + dx) % 4) * 2 + (ic ^ dc)))
        return lax.ppermute(a, "fsdp", pairs)

    line = jnp.concatenate([w, to(w, 1, 0), to(w, -1, 0), to(w, 2, 0)], axis=0)
    own = jnp.concatenate([line, to(line, 0, 1), to(line, 0, -1), to(line, 0, 2)], axis=0)
    other = to(own, 0, 0, 1)
    home = [
        ((z + dz) % 4) * 8 + ((x + dx) % 4) * 2 + (c ^ dc)
        for dc in range(2)
        for dx in (0, -1, 1, 2)
        for dz in (0, -1, 1, 2)
    ]
    return line, own, other, jnp.stack(home)


HEAD = 40


def on_device(hidden, token_ids, table, gain_hidden, gain_embed, proj_hidden, proj_embed):
    width = gain_hidden.shape[0]
    tokens, block = hidden.shape
    rows, out_width = proj_hidden.shape
    sections = lax.axis_size("section")
    groups = lax.axis_size("fsdp")
    section = lax.axis_index("section")
    cut = HEAD - rows

    ids = lax.all_to_all(
        jnp.broadcast_to(token_ids[None], (groups, tokens)), "fsdp", split_axis=0, concat_axis=0, tiled=True
    )
    main = lax.all_gather(jnp.concatenate([proj_hidden, proj_embed[:cut]], axis=0), "fsdp", axis=0, tiled=True)
    line, own, other, home = spread(proj_embed[cut:])

    f, r = jnp.arange(groups)[:, None], jnp.arange(HEAD)[None, :]
    source = jnp.where(r < rows, groups * PAD + f * rows + r, f * PAD + r - rows)
    tail = home[:, None] * PAD + cut + jnp.arange(rows - cut)[None, :]
    source = jnp.concatenate([source.reshape(-1), tail.reshape(-1)])[None, :]
    is_hidden = (source >= groups * PAD).astype(f32)
    gain_h = lax.dynamic_slice_in_dim(gain_hidden, section * block, block).reshape(groups, rows)
    gain_e = lax.dynamic_slice_in_dim(gain_embed, section * block, block).reshape(groups, rows)
    gain_t = jnp.sum(jnp.where(home[:, None, None] == f[None], gain_e[None, :, cut:], 0.0), axis=1)
    gain = jnp.concatenate(
        [jnp.concatenate([gain_h, gain_e[:, :cut]], axis=1).reshape(-1), gain_t.reshape(-1)]
    )[None, :]
    hf = hidden.astype(f32)
    h_sq = jnp.sum(hf * hf, axis=1)

    turned = turn(table)
    ids, line = lax.optimization_barrier((ids, line))
    ids = jnp.roll(ids.reshape(-1), -1).reshape(groups, tokens)
    looked = look(turned, ids)
    e = lax.all_to_all(looked, "fsdp", split_axis=0, concat_axis=0, tiled=True)
    ef = e.astype(f32)
    squares = jnp.stack([h_sq, jnp.sum(ef * ef, axis=(0, 1))])
    squares = lax.all_to_all(
        jnp.broadcast_to(squares[None], (sections, 2, tokens)), "section", split_axis=0, concat_axis=0, tiled=True
    )
    scales = lax.rsqrt(jnp.sum(squares, axis=0) / width + EPS)
    x = prep(hidden, e, source)
    sums = mix(x, gain, is_hidden, scales, [main, own, other], sections)
    got = lax.all_to_all(sums, "section", split_axis=0, concat_axis=0, tiled=True)
    return add_parts(got)


def solution(mesh):
    placed = (
        P("fsdp", "section"),
        P("fsdp"),
        P(("section", "fsdp"), None),
        P(),
        P(),
        P(("section", "fsdp"), None),
        P(("section", "fsdp"), None),
    )
    return jax.shard_map(
        on_device, mesh=mesh, in_specs=placed, out_specs=P("fsdp", "section"), check_vma=False
    )
```

time: 529 us -> 221 us (0.42)
  waiting for transfers between devices: 228 us -> 37.7 us
  local copies, waits for them, and re-layouts: 161 us -> 21.3 us
  Pallas kernels: 0 us -> 53 us
  blocking collectives: 87.6 us -> 54.8 us
  starting transfers between devices: 9.2 us -> 33.5 us
  matrix products: 18.5 us -> 0 us
    all_gather x4 -> x1, waiting for transfers between devices: 202 us -> 0.01 us  [on_device(): lax.all_gather(jnp.concatenate([proj_hidden, proj_embed[:cut]], axis=0),...]
    gather x2 -> x0, local copies, waits for them, and re-layouts: 67 us -> none  [on_device(): looked = jnp.take(table, shifted, axis=1)]
    pallas_call x0 -> x5, Pallas kernels: none -> 53 us  [the longest x1 21.6 us: look(): pl.pallas_call(functools.partial(look_kernel, quarter), out_shape=jax.Sha...]
    reshape x4, local copies, waits for them, and re-layouts: 46.2 us -> 0.36 us  [the longest x1 0.1 us: on_device(): lax.dynamic_slice_in_dim(gain_embed, section * block, block)]
    all_gather x1 -> x0, blocking collectives: 42.8 us -> none  [on_device(): every_id = lax.all_gather(token_ids, 'fsdp', axis=0, tiled=True)]
    all_to_all x2 -> x1, blocking collectives: 25 us -> 54.8 us  [on_device(): lax.all_to_all(sums, 'section', split_axis=0, concat_axis=0, tiled=True)]
    psum x1 -> x0, blocking collectives: 19.9 us -> none  [on_device(): lax.psum((jnp.sum(hidden_f * hidden_f, axis=1), jnp.sum(embed_f * embed_f...]
    dot_general x2 -> x0, matrix products: 18.5 us -> none  [the longest x1 10 us: on_device(): lax.dot_general(right, pieces[1], (((0,), (0,)), ((), ())), preferred_ele...]
  transfers between devices with their start and end apart: 5 -> 11, of which waited for: 5 -> 2; matrix products, arithmetic and copies ran while one was open for 17% -> 9% of each run, Pallas kernels for 0% -> 16%
where the time goes in v2:
time: 221 us; the launch traced here: 220 us
  blocking collectives  54.8 us (25%)
  Pallas kernels  53 us (24%)
  waiting for transfers between devices  37.7 us (17%)
  starting transfers between devices  33.5 us (15%)
  local copies, waits for them, and re-layouts  21.3 us (10%)
  between operations  13.8 us (6%)
  other arithmetic  5.75 us (3%)
    all_to_all x1, blocking collectives, on_device(): lax.all_to_all(sums, 'section', split_axis=0, concat_axis=0, tiled=True)  54.8 us
    all_to_all x1, waiting for transfers between devices, on_device(): e = lax.all_to_all(looked, 'fsdp', split_axis=0, concat_axis=0, tiled=True)  35.4 us
    pallas_call x1, Pallas kernels, look(): pl.pallas_call(functools.partial(look_kernel, quarter), out_shape=jax.Sha...  21.6 us
    ppermute x7, starting transfers between devices, to(): return lax.ppermute(a, 'fsdp', pairs)  15.4 us
    pallas_call x1, Pallas kernels, mix(): pl.pallas_call(functools.partial(mix_kernel, len(pieces)), out_shape=jax....  14.6 us
    unnamed x24, local copies, waits for them, and re-layouts  13.9 us
    all_to_all x1, starting transfers between devices, on_device(): e = lax.all_to_all(looked, 'fsdp', split_axis=0, concat_axis=0, tiled=True)  7.44 us
    pallas_call x1, Pallas kernels, turn(): pl.pallas_call(turn_kernel, out_shape=jax.ShapeDtypeStruct((quarter, LANE...  7.29 us
  transfers between devices with their start and end apart: 11, of which 2 were waited for; matrix products, arithmetic and copies ran while one was open for 9% of the time, Pallas kernels for 16%

profile of v2, /device:TPU:2, one launch (start us, length us, event | category | flops | bytes accessed | tf_op | source)
XLA Modules:
  0.0 219.9 jit_solution(13984277816484936451)
XLA Ops:
  7.5 1.7 pad_maximum_fusion.1
  9.2 1.6 constant_dynamic-update-slice_fusion.6
  10.8 3.3 %collective-permute-start = (bf16[16,4096]{1,0:T(8,128)(2,1)S(1)}, bf16[16,4096]{1,0:T(8,128)(2,1)S(1)}, u32[]{:S(2)}, u32[]{:S(2)}) collective-permute-start(bf16[16,4096]{1,0:T(8,128)(2,1)S(1)} %get-tuple-element.10), channel_id=1, source_target_pairs={{0,8},{1,9},{2,10},{3,11},{4,12},{5,13},{6,14},{7,15},{8,16},{9,17... | collective-permute-start | bytes 393224 | tf_op jit(solution)/shard_map/ppermute | solution.py:195
  14.1 3.0 %collective-permute-start.1 = (bf16[16,4096]{1,0:T(8,128)(2,1)S(1)}, bf16[16,4096]{1,0:T(8,128)(2,1)S(1)}, u32[]{:S(2)}, u32[]{:S(2)}) collective-permute-start(bf16[16,4096]{1,0:T(8,128)(2,1)S(1)} %get-tuple-element.10), channel_id=1, source_target_pairs={{0,24},{1,25},{2,26},{3,27},{4,28},{5,29},{6,30},{7,31},{8,0},{9,1... | collective-permute-start | bytes 393224 | tf_op jit(solution)/shard_map/ppermute | solution.py:195
  17.1 5.0 %collective-permute-start.2 = (bf16[16,4096]{1,0:T(8,128)(2,1)S(1)}, bf16[16,4096]{1,0:T(8,128)(2,1)S(1)}, u32[]{:S(2)}, u32[]{:S(2)}) collective-permute-start(bf16[16,4096]{1,0:T(8,128)(2,1)S(1)} %get-tuple-element.10), channel_id=1, source_target_pairs={{0,16},{1,17},{2,18},{3,19},{4,20},{5,21},{6,22},{7,23},{8,24},{9,... | collective-permute-start | bytes 393224 | tf_op jit(solution)/shard_map/ppermute | solution.py:195
  22.1 1.3 broadcast_in_dim.54
  23.5 5.3 %all-to-all-start = ((s32[32,1,512]{2,1,0:T(1,128)}), s32[32,1,512]{2,1,0:T(1,128)S(1)}, u32[]{:S(2)}, u32[]{:S(2)}) async-start(s32[32,1,512]{2,1,0:T(1,128)} %broadcast_in_dim.54), calls=%async_computation | async-start | bytes 131072 | tf_op jit(solution)/shard_map/all_to_all | solution.py:221
  29.4 7.3 %turn.1 = f32[16384,128]{1,0:T(8,128)} custom-call(bf16[28,65536]{1,0:T(8,128)(2,1)} %refs_3_.1, bf16[28,65536]{1,0:T(8,128)(2,1)} %refs_3_.1, bf16[28,65536]{1,0:T(8,128)(2,1)} %refs_3_.1, bf16[28,65536]{1,0:T(8,128)(2,1)} %refs_3_.1), custom_call_target="tpu_custom_call" | custom-call | bytes 11010048 | tf_op jit(solution)/shard_map/turn/pallas_call | solution.py:39
  37.2 2.3 %all-to-all-done = s32[32,1,512]{2,1,0:T(1,128)S(1)} async-done(((s32[32,1,512]{2,1,0:T(1,128)}), s32[32,1,512]{2,1,0:T(1,128)S(1)}, u32[]{:S(2)}, u32[]{:S(2)}) %all-to-all-start) | async-done | bytes 65568 | tf_op jit(solution)/shard_map/all_to_all | solution.py:221
  40.4 1.3 collective-permute-start.3
  42.4 2.0 collective-permute-start.5
  45.5 3.4 %copy-done = f32[16384,128]{1,0:T(8,128)S(1)} copy-done((f32[16384,128]{1,0:T(8,128)S(1)}, f32[16384,128]{1,0:T(8,128)}, u32[]{:S(2)}) %copy-start) | copy-done | bytes 8388632
  48.9 21.6 %look.1 = bf16[32,32,512]{2,1,0:T(8,128)(2,1)} custom-call(s32[32,1,512]{2,1,0:T(1,128)S(1)} %and_select_fusion.1.row_ref, s32[32,1,512]{2,1,0:T(1,128)S(1)} %get-tuple-element.7.grp_ref, f32[16384,1,128]{2,1,0:T(1,128)S(1)} %bitcast.42), custom_call_target="tpu_custom_call" | custom-call | tf_op jit(solution)/shard_map/look/pallas_call | solution.py:74
  70.5 7.4 %all-to-all-start.1 = ((bf16[32,32,512]{2,1,0:T(8,128)(2,1)}), bf16[32,32,512]{2,1,0:T(8,128)(2,1)S(1)}, u32[]{:S(2)}, u32[]{:S(2)}) async-start(bf16[32,32,512]{2,1,0:T(8,128)(2,1)} %look.1), calls=%async_computation.1 | async-start | bytes 2097152 | tf_op jit(solution)/shard_map/all_to_all | solution.py:245
  78.0 1.7 constant_dynamic-update-slice_fusion.5
  79.6 1.6 constant_dynamic-update-slice_fusion.4
  81.3 1.6 constant_dynamic-update-slice_fusion.3
  82.8 1.9 constant_dynamic-update-slice_fusion.2
  90.7 35.4 %all-to-all-done.1.e_ref = bf16[32,32,512]{2,1,0:T(8,128)(2,1)S(1)} async-done(((bf16[32,32,512]{2,1,0:T(8,128)(2,1)}), bf16[32,32,512]{2,1,0:T(8,128)(2,1)S(1)}, u32[]{:S(2)}, u32[]{:S(2)}) %all-to-all-start.1) | async-done | bytes 1048608 | tf_op jit(solution)/shard_map/all_to_all | solution.py:245
  126.9 5.3 %all-to-all-start.2 = ((f32[8,2,512]{2,1,0:T(2,128)}), f32[8,2,512]{2,1,0:T(2,128)S(1)}, u32[]{:S(2)}, u32[]{:S(2)}) async-start(f32[8,2,512]{2,1,0:T(2,128)} %broadcast_in_dim.61), calls=%async_computation.2 | async-start | bytes 65536 | tf_op jit(solution)/shard_map/all_to_all | solution.py:248
  132.3 5.4 %prep.1.refs_0_ = bf16[512,1792]{1,0:T(8,128)(2,1)S(1)} custom-call(bf16[512,896]{1,0:T(8,128)(2,1)S(1)} %copy-done.1, bf16[32,32,512]{2,1,0:T(8,128)(2,1)S(1)} %all-to-all-done.1.e_ref, s32[1,1792]{1,0:T(1,128)S(1)} %broadcast_in_dim.56.s_ref), custom_call_target="tpu_custom_call" | custom-call | flops 3523215360 | bytes 8388608 | tf_op jit(solution)/shard_map/prep/pallas_call | solution.py:113
  139.6 14.6 %mix.1 = bf16[8,512,512]{2,1,0:T(8,128)(2,1)} custom-call(bf16[512,1792]{1,0:T(8,128)(2,1)} %copy-done.2, f32[1,1792]{1,0:T(1,128)} %broadcast_in_dim.60.refs_1_, f32[1,1792]{1,0:T(1,128)} %compare_convert_fusion.refs_2_, f32[2,512]{1,0:T(2,128)} %add_rsqrt_fusion.refs_3_, bf16[1280,4096]{1,0:T(8,128)(2,1)} %all-gather.2.cloned.1.call-done.refs_4_, ...), custom_call_target="tpu_custom_call" | custom-call | flops 7516192768 | bytes 29360128 | tf_op jit(solution)/shard_map/mix/pallas_call | solution.py:151
  154.2 54.8 %all_to_all.24.x_ref = bf16[8,512,512]{2,1,0:T(8,128)(2,1)} all-to-all(bf16[8,512,512]{2,1,0:T(8,128)(2,1)} %mix.1), channel_id=1, replica_groups=mesh['section'=8,'fsdp'=32] {'section'}, dimensions={0} | all-to-all | bytes 8388608 | tf_op jit(solution)/shard_map/all_to_all | solution.py:254
  209.0 4.1 %add_parts.1 = bf16[512,512]{1,0:T(8,128)(2,1)} custom-call(bf16[8,512,512]{2,1,0:T(8,128)(2,1)} %all_to_all.24.x_ref), custom_call_target="tpu_custom_call" | custom-call | tf_op jit(solution)/shard_map/add_parts/pallas_call | solution.py:176
  (71 shorter events, 13.1 us)
Async XLA Ops:
  6.5 133.0 %all-gather.2.cloned.1.call-start = ((), (), s32[]{:S(2)}) async-start(), calls=%async_computation.4 | async-start | bytes 10813440 | tf_op jit(solution)/shard_map/all_gather | solution.py:224
  10.8 28.8 %collective-permute-start = (bf16[16,4096]{1,0:T(8,128)(2,1)S(1)}, bf16[16,4096]{1,0:T(8,128)(2,1)S(1)}, u32[]{:S(2)}, u32[]{:S(2)}) collective-permute-start(bf16[16,4096]{1,0:T(8,128)(2,1)S(1)} %get-tuple-element.10), channel_id=1, source_target_pairs={{0,8},{1,9},{2,10},{3,11},{4,12},{5,13},{6,14},{7,15},{8,16},{9,17... | collective-permute-start | bytes 393224 | tf_op jit(solution)/shard_map/ppermute | solution.py:195
  14.1 25.5 %collective-permute-start.1 = (bf16[16,4096]{1,0:T(8,128)(2,1)S(1)}, bf16[16,4096]{1,0:T(8,128)(2,1)S(1)}, u32[]{:S(2)}, u32[]{:S(2)}) collective-permute-start(bf16[16,4096]{1,0:T(8,128)(2,1)S(1)} %get-tuple-element.10), channel_id=1, source_target_pairs={{0,24},{1,25},{2,26},{3,27},{4,28},{5,29},{6,30},{7,31},{8,0},{9,1... | collective-permute-start | bytes 393224 | tf_op jit(solution)/shard_map/ppermute | solution.py:195
  17.1 22.5 %collective-permute-start.2 = (bf16[16,4096]{1,0:T(8,128)(2,1)S(1)}, bf16[16,4096]{1,0:T(8,128)(2,1)S(1)}, u32[]{:S(2)}, u32[]{:S(2)}) collective-permute-start(bf16[16,4096]{1,0:T(8,128)(2,1)S(1)} %get-tuple-element.10), channel_id=1, source_target_pairs={{0,16},{1,17},{2,18},{3,19},{4,20},{5,21},{6,22},{7,23},{8,24},{9,... | collective-permute-start | bytes 393224 | tf_op jit(solution)/shard_map/ppermute | solution.py:195
  23.5 16.1 %all-to-all-start = ((s32[32,1,512]{2,1,0:T(1,128)}), s32[32,1,512]{2,1,0:T(1,128)S(1)}, u32[]{:S(2)}, u32[]{:S(2)}) async-start(s32[32,1,512]{2,1,0:T(1,128)} %broadcast_in_dim.54), calls=%async_computation | async-start | bytes 131072 | tf_op jit(solution)/shard_map/all_to_all | solution.py:221
  39.6 30.9 %copy-start.3 = (bf16[16,4096]{1,0:T(8,128)(2,1)}, bf16[16,4096]{1,0:T(8,128)(2,1)S(1)}, u32[]{:S(2)}) copy-start(bf16[16,4096]{1,0:T(8,128)(2,1)S(1)} %collective-permute-done) | copy-start | bytes 393220
  39.6 30.9 %copy-start.4 = (bf16[16,4096]{1,0:T(8,128)(2,1)}, bf16[16,4096]{1,0:T(8,128)(2,1)S(1)}, u32[]{:S(2)}) copy-start(bf16[16,4096]{1,0:T(8,128)(2,1)S(1)} %collective-permute-done.1) | copy-start | bytes 393220
  39.6 30.9 %copy-start.5 = (bf16[16,4096]{1,0:T(8,128)(2,1)}, bf16[16,4096]{1,0:T(8,128)(2,1)S(1)}, u32[]{:S(2)}) copy-start(bf16[16,4096]{1,0:T(8,128)(2,1)S(1)} %collective-permute-done.2) | copy-start | bytes 393220
  40.4 42.5 %collective-permute-start.3 = (bf16[64,4096]{1,0:T(8,128)(2,1)S(1)}, bf16[64,4096]{1,0:T(8,128)(2,1)}, u32[]{:S(2)}, u32[]{:S(2)}) collective-permute-start(bf16[64,4096]{1,0:T(8,128)(2,1)S(1)} %pad_maximum_fusion), channel_id=1, source_target_pairs={{0,2},{1,3},{2,4},{3,5},{4,6},{5,7},{6,0},{7,1},{8,10},{9,11},{10,... | collective-permute-start | bytes 1572872 | tf_op jit(solution)/shard_map/ppermute | solution.py:195
  41.7 43.0 %collective-permute-start.4 = (bf16[64,4096]{1,0:T(8,128)(2,1)S(1)}, bf16[64,4096]{1,0:T(8,128)(2,1)S(1)}, u32[]{:S(2)}, u32[]{:S(2)}) collective-permute-start(bf16[64,4096]{1,0:T(8,128)(2,1)S(1)} %pad_maximum_fusion), channel_id=1, source_target_pairs={{0,6},{1,7},{2,0},{3,1},{4,2},{5,3},{6,4},{7,5},{8,14},{9,15},{10,... | collective-permute-start | bytes 1572872 | tf_op jit(solution)/shard_map/ppermute | solution.py:195
  42.4 43.2 %collective-permute-start.5 = (bf16[64,4096]{1,0:T(8,128)(2,1)S(1)}, bf16[64,4096]{1,0:T(8,128)(2,1)S(1)}, u32[]{:S(2)}, u32[]{:S(2)}) collective-permute-start(bf16[64,4096]{1,0:T(8,128)(2,1)S(1)} %pad_maximum_fusion), channel_id=1, source_target_pairs={{0,4},{1,5},{2,6},{3,7},{4,0},{5,1},{6,2},{7,3},{8,12},{9,13},{10,... | collective-permute-start | bytes 1572872 | tf_op jit(solution)/shard_map/ppermute | solution.py:195
  45.5 3.4 %copy-start = (f32[16384,128]{1,0:T(8,128)S(1)}, f32[16384,128]{1,0:T(8,128)}, u32[]{:S(2)}) copy-start(f32[16384,128]{1,0:T(8,128)} %turn.1) | copy-start | bytes 25165828
  70.5 55.5 %all-to-all-start.1 = ((bf16[32,32,512]{2,1,0:T(8,128)(2,1)}), bf16[32,32,512]{2,1,0:T(8,128)(2,1)S(1)}, u32[]{:S(2)}, u32[]{:S(2)}) async-start(bf16[32,32,512]{2,1,0:T(8,128)(2,1)} %look.1), calls=%async_computation.1 | async-start | bytes 2097152 | tf_op jit(solution)/shard_map/all_to_all | solution.py:245
  78.0 8.6 %copy-start.6 = (s32[32]{0:T(128)S(1)}, s32[32]{0:T(128)}, u32[]{:S(2)}) copy-start(s32[32]{0:T(128)} %get-tuple-element.11) | copy-start | bytes 388
  78.0 8.5 %copy-start.7 = (s32[32]{0:T(128)S(1)}, s32[32]{0:T(128)}, u32[]{:S(2)}) copy-start(s32[32]{0:T(128)} %get-tuple-element.12) | copy-start | bytes 388
  78.0 11.8 %copy-start.1 = (bf16[512,896]{1,0:T(8,128)(2,1)S(1)}, bf16[512,896]{1,0:T(8,128)(2,1)}, u32[]{:S(2)}) copy-start(bf16[512,896]{1,0:T(8,128)(2,1)} %h_ref.1) | copy-start | bytes 2752516
  86.4 53.2 %collective-permute-start.6 = (bf16[256,4096]{1,0:T(8,128)(2,1)}, bf16[256,4096]{1,0:T(8,128)(2,1)}, u32[]{:S(2)}, u32[]{:S(2)}) collective-permute-start(bf16[256,4096]{1,0:T(8,128)(2,1)} %constant_dynamic-update-slice_fusion.refs_5_), channel_id=1, source_target_pairs={{0,1},{1,0},{2,3},{3,2},{4,5},{5,4},{6,7},{7,6},{8,9},{9,8},{10,11... | collective-permute-start | bytes 6291464 | tf_op jit(solution)/shard_map/ppermute | solution.py:195
  126.9 12.0 %all-to-all-start.2 = ((f32[8,2,512]{2,1,0:T(2,128)}), f32[8,2,512]{2,1,0:T(2,128)S(1)}, u32[]{:S(2)}, u32[]{:S(2)}) async-start(f32[8,2,512]{2,1,0:T(2,128)} %broadcast_in_dim.61), calls=%async_computation.2 | async-start | bytes 65536 | tf_op jit(solution)/shard_map/all_to_all | solution.py:248
  137.7 1.3 copy-start.2
Sparse Core Ops, SparseCore 0:
  9.9 109.7 all-gather.1

commit v3 on v2

--- a/solution.py
+++ b/solution.py
@@ -43,7 +43,6 @@
         in_specs=[pl.BlockSpec((rows, cols), functools.partial(lambda g, i: (0, g * per + i), g)) for g in range(FOLD)],
         out_specs=pl.BlockSpec((cols, LANES), lambda i: (i, 0)),
         compiler_params=pltpu.CompilerParams(vmem_limit_bytes=60 << 20),
-        cost_estimate=pl.CostEstimate(flops=0, bytes_accessed=3 * rows * vocab * 2, transcendentals=0),
         name="turn",
     )(*[table] * FOLD)
 
@@ -120,12 +119,14 @@
     )(h, e, source)
 
 
-def mix_kernel(n_pieces, *refs):
+def mix_kernel(n_pieces, order_ref, *refs):
     x_ref, g_ref, m_ref, s_ref = refs[:4]
     pieces = refs[4 : 4 + n_pieces]
-    out_ref, left_ref = refs[4 + n_pieces :]
-
-    @pl.when(pl.program_id(0) == 0)
+    a_send, a_keep, b_1, b_2, b_3, b_keep, left_ref = refs[4 + n_pieces :]
+    n = pl.program_id(0)
+    side = n % 4
+
+    @pl.when(n == 0)
     def _():
         tokens, depth = x_ref.shape
         scale_h = jnp.broadcast_to(s_ref[0:1], (LANES, tokens)).T
@@ -141,46 +142,101 @@
         term = jnp.dot(left_ref[:, at : at + rows], p[...], preferred_element_type=f32)
         acc = term if acc is None else acc + term
         at += rows
-    out_ref[0] = acc.astype(bf)
+    half = acc.shape[1] // 2
+
+    @pl.when(n < 4)
+    def _():
+        a_send[0] = acc[:, :half].astype(bf)
+
+    @pl.when(n >= 4)
+    def _():
+        a_keep[0] = acc[:, :half]
+
+    for i, ref in enumerate((b_1, b_2, b_3, b_keep)):
+
+        @pl.when(side == i)
+        def _():
+            ref[0] = acc[:, half:].astype(ref.dtype)
 
 
 def mix(x, gain, is_hidden, scales, pieces, sections):
     tokens, depth = x.shape
     cols = pieces[0].shape[1] // sections
-    whole = lambda n: (0, 0)
+    half = cols // 2
+    section = lax.axis_index("section")
+    z, y = section // 4, section % 4
+    order = jnp.stack([(zz * 4 + (y + 1 + i) % 4) for zz in (1 - z, z) for i in range(4)])
+    whole = lambda n, order: (0, 0)
+    block = lambda place: pl.BlockSpec((1, tokens, half), lambda n, order: (place(n), 0, 0))
+    shape = lambda count, kind: jax.ShapeDtypeStruct((count, tokens, half), kind)
+    later = lambda i: lambda n: jnp.where(n < 4 + i, 0, 1)
     return pl.pallas_call(
         functools.partial(mix_kernel, len(pieces)),
-        out_shape=jax.ShapeDtypeStruct((sections, tokens, cols), bf),
-        grid=(sections,),
-        in_specs=[pl.BlockSpec(a.shape, whole) for a in (x, gain, is_hidden, scales)]
-        + [pl.BlockSpec((p.shape[0], cols), lambda n: (0, n)) for p in pieces],
-        out_specs=pl.BlockSpec((1, tokens, cols), lambda n: (n, 0, 0)),
-        scratch_shapes=[pltpu.VMEM((tokens, depth), bf)],
-        compiler_params=pltpu.CompilerParams(vmem_limit_bytes=60 << 20),
+        out_shape=[shape(4, bf), shape(4, f32), shape(2, bf), shape(2, bf), shape(2, bf), shape(2, f32)],
+        grid_spec=pltpu.PrefetchScalarGridSpec(
+            num_scalar_prefetch=1,
+            grid=(sections,),
+            in_specs=[pl.BlockSpec(a.shape, whole) for a in (x, gain, is_hidden, scales)]
+            + [pl.BlockSpec((p.shape[0], cols), lambda n, order: (0, order[n])) for p in pieces],
+            out_specs=[block(lambda n: jnp.minimum(n, 3)), block(lambda n: jnp.maximum(n - 4, 0))]
+            + [block(later(i)) for i in range(4)],
+            scratch_shapes=[pltpu.VMEM((tokens, depth), bf)],
+        ),
+        compiler_params=pltpu.CompilerParams(vmem_limit_bytes=50 << 20),
         cost_estimate=pl.CostEstimate(
             flops=2 * tokens * depth * cols * sections, bytes_accessed=4 * depth * cols * sections, transcendentals=0
         ),
         name="mix",
-    )(x, gain, is_hidden, scales, *pieces)
-
-
-def add_kernel(x_ref, out_ref):
-    total = x_ref[0].astype(f32)
-    for i in range(1, x_ref.shape[0]):
-        total = total + x_ref[i].astype(f32)
-    out_ref[...] = total.astype(bf)
-
-
-def add_parts(x, step=128):
-    parts, tokens, cols = x.shape
-    return pl.pallas_call(
-        add_kernel,
-        out_shape=jax.ShapeDtypeStruct((tokens, cols), bf),
+    )(order, x, gain, is_hidden, scales, *pieces)
+
+
+def fold_kernel(a_keep, a_in, b_keep, b_1, b_2, b_3, a_1, a_2, a_3, a_own, b_send, b_own):
+    for i, ref in enumerate((a_1, a_2, a_3, a_own)):
+        ref[...] = (a_keep[i] + a_in[i].astype(f32)).astype(ref.dtype)
+    for i, ref in enumerate((b_send, b_own)):
+        total = b_keep[i] + b_1[i].astype(f32) + b_2[i].astype(f32) + b_3[i].astype(f32)
+        ref[...] = total.astype(ref.dtype)
+
+
+def last_kernel(a_own, a_1, a_2, a_3, b_own, b_in, out_ref):
+    half = a_own.shape[1]
+    out_ref[:, :half] = (a_own[...] + a_1[...].astype(f32) + a_2[...].astype(f32) + a_3[...].astype(f32)).astype(bf)
+    out_ref[:, half:] = (b_own[...] + b_in[...].astype(f32)).astype(bf)
+
+
+def fold(a_send, a_keep, b_1, b_2, b_3, b_keep, step=128):
+    count = lax.axis_size("section")
+    _, tokens, half = a_keep.shape
+
+    def to(a, dz, dy):
+        pairs = [(i, ((i // 4 + dz) % 2) * 4 + (i % 4 + dy) % 4) for i in range(count)]
+        return lax.ppermute(a, "section", pairs)
+
+    b_in = [to(b, 0, d) for b, d in ((b_1, 1), (b_2, 2), (b_3, 3))]
+    a_in = to(a_send, 1, 0)
+    deep = lambda n: pl.BlockSpec((n, step, half), lambda i: (0, i, 0))
+    flat = pl.BlockSpec((step, half), lambda i: (i, 0))
+    shape = lambda kind: jax.ShapeDtypeStruct((tokens, half), kind)
+    a_1, a_2, a_3, a_own, b_send, b_own = pl.pallas_call(
+        fold_kernel,
+        out_shape=[shape(bf)] * 3 + [shape(f32), shape(bf), shape(f32)],
         grid=(tokens // step,),
-        in_specs=[pl.BlockSpec((parts, step, cols), lambda i: (0, i, 0))],
-        out_specs=pl.BlockSpec((step, cols), lambda i: (i, 0)),
-        name="add_parts",
-    )(x)
+        in_specs=[deep(4), deep(4), deep(2), deep(2), deep(2), deep(2)],
+        out_specs=[flat] * 6,
+        compiler_params=pltpu.CompilerParams(vmem_limit_bytes=16 << 20),
+        name="fold",
+    )(a_keep, a_in, b_keep, *b_in)
+    a_more = [to(a, 0, d) for a, d in ((a_1, 1), (a_2, 2), (a_3, 3))]
+    b_more = to(b_send, 1, 0)
+    return pl.pallas_call(
+        last_kernel,
+        out_shape=jax.ShapeDtypeStruct((tokens, 2 * half), bf),
+        grid=(tokens // step,),
+        in_specs=[flat] * 6,
+        out_specs=pl.BlockSpec((step, 2 * half), lambda i: (i, 0)),
+        compiler_params=pltpu.CompilerParams(vmem_limit_bytes=16 << 20),
+        name="last",
+    )(a_own, *a_more, b_own, b_more)
 
 
 def spread(w):
@@ -196,14 +252,14 @@
 
     line = jnp.concatenate([w, to(w, 1, 0), to(w, -1, 0), to(w, 2, 0)], axis=0)
     own = jnp.concatenate([line, to(line, 0, 1), to(line, 0, -1), to(line, 0, 2)], axis=0)
-    other = to(own, 0, 0, 1)
+    pieces = [own, to(own, 0, 0, 1)]
     home = [
         ((z + dz) % 4) * 8 + ((x + dx) % 4) * 2 + (c ^ dc)
         for dc in range(2)
         for dx in (0, -1, 1, 2)
         for dz in (0, -1, 1, 2)
     ]
-    return line, own, other, jnp.stack(home)
+    return line, pieces, jnp.stack(home)
 
 
 HEAD = 40
@@ -216,43 +272,42 @@
     sections = lax.axis_size("section")
     groups = lax.axis_size("fsdp")
     section = lax.axis_index("section")
-    cut = HEAD - rows
+    both = jnp.concatenate([proj_hidden, proj_embed], axis=0)
+    depth = 2 * rows
 
     ids = lax.all_to_all(
         jnp.broadcast_to(token_ids[None], (groups, tokens)), "fsdp", split_axis=0, concat_axis=0, tiled=True
     )
-    main = lax.all_gather(jnp.concatenate([proj_hidden, proj_embed[:cut]], axis=0), "fsdp", axis=0, tiled=True)
-    line, own, other, home = spread(proj_embed[cut:])
-
-    f, r = jnp.arange(groups)[:, None], jnp.arange(HEAD)[None, :]
-    source = jnp.where(r < rows, groups * PAD + f * rows + r, f * PAD + r - rows)
-    tail = home[:, None] * PAD + cut + jnp.arange(rows - cut)[None, :]
-    source = jnp.concatenate([source.reshape(-1), tail.reshape(-1)])[None, :]
+    main = lax.all_gather(both[:HEAD], "fsdp", axis=0, tiled=True)
+
+    turned = turn(table)
+    ids = jnp.roll(ids.reshape(-1), -1).reshape(groups, tokens)
+    looked = look(turned, ids)
+    tail_rows = both[HEAD:]
+    e = lax.all_to_all(looked, "fsdp", split_axis=0, concat_axis=0, tiled=True)
+    line, pieces, home = spread(tail_rows)
+
+    f, r = jnp.arange(groups)[:, None], jnp.arange(depth)[None, :]
+
+    def place(f, r):
+        return jnp.where(r < rows, groups * PAD + f * rows + r, f * PAD + r - rows).reshape(-1)
+
+    source = jnp.concatenate([place(f, r[:, :HEAD]), place(home[:, None], r[:, HEAD:])])[None, :]
     is_hidden = (source >= groups * PAD).astype(f32)
     gain_h = lax.dynamic_slice_in_dim(gain_hidden, section * block, block).reshape(groups, rows)
     gain_e = lax.dynamic_slice_in_dim(gain_embed, section * block, block).reshape(groups, rows)
-    gain_t = jnp.sum(jnp.where(home[:, None, None] == f[None], gain_e[None, :, cut:], 0.0), axis=1)
-    gain = jnp.concatenate(
-        [jnp.concatenate([gain_h, gain_e[:, :cut]], axis=1).reshape(-1), gain_t.reshape(-1)]
-    )[None, :]
+    gains = jnp.concatenate([gain_h, gain_e], axis=1)
+    gain_t = jnp.sum(jnp.where(home[:, None, None] == f[None], gains[None, :, HEAD:], 0.0), axis=1)
+    gain = jnp.concatenate([gains[:, :HEAD].reshape(-1), gain_t.reshape(-1)])[None, :]
     hf = hidden.astype(f32)
-    h_sq = jnp.sum(hf * hf, axis=1)
-
-    turned = turn(table)
-    ids, line = lax.optimization_barrier((ids, line))
-    ids = jnp.roll(ids.reshape(-1), -1).reshape(groups, tokens)
-    looked = look(turned, ids)
-    e = lax.all_to_all(looked, "fsdp", split_axis=0, concat_axis=0, tiled=True)
     ef = e.astype(f32)
-    squares = jnp.stack([h_sq, jnp.sum(ef * ef, axis=(0, 1))])
+    squares = jnp.stack([jnp.sum(hf * hf, axis=1), jnp.sum(ef * ef, axis=(0, 1))])
     squares = lax.all_to_all(
         jnp.broadcast_to(squares[None], (sections, 2, tokens)), "section", split_axis=0, concat_axis=0, tiled=True
     )
     scales = lax.rsqrt(jnp.sum(squares, axis=0) / width + EPS)
     x = prep(hidden, e, source)
-    sums = mix(x, gain, is_hidden, scales, [main, own, other], sections)
-    got = lax.all_to_all(sums, "section", split_axis=0, concat_axis=0, tiled=True)
-    return add_parts(got)
+    return fold(*mix(x, gain, is_hidden, scales, [main] + pieces, sections))
 
 
 def solution(mesh):

time: 221 us -> 208 us (0.941)
  blocking collectives: 54.8 us -> 0 us
  waiting for transfers between devices: 37.7 us -> 76.4 us
  starting transfers between devices: 33.5 us -> 43 us
  local copies, waits for them, and re-layouts: 21.3 us -> 17.7 us
    all_to_all x1 -> x0, blocking collectives: 54.8 us -> none  [on_device(): lax.all_to_all(sums, 'section', split_axis=0, concat_axis=0, tiled=True)]
    ppermute x7, waiting for transfers between devices: 0.02 us -> 39.4 us  [to(): return lax.ppermute(a, 'fsdp', pairs)]
    all_to_all x1, waiting for transfers between devices: 35.4 us -> 2.24 us  [on_device(): e = lax.all_to_all(looked, 'fsdp', split_axis=0, concat_axis=0, tiled=True)]
    ppermute x0 -> x8, waiting for transfers between devices: none -> 32 us  [to(): return lax.ppermute(a, 'section', pairs)]
    ppermute x0 -> x8, starting transfers between devices: none -> 10.9 us  [to(): return lax.ppermute(a, 'section', pairs)]
    unnamed x24 -> x13, local copies, waits for them, and re-layouts: 13.9 us -> 9.91 us
    pallas_call x2 -> x3, Pallas kernels: 18.7 us -> 17.4 us  [the longest x1 15 us: mix(): pl.pallas_call(functools.partial(mix_kernel, len(pieces)), out_shape=[sha...]
  transfers between devices with their start and end apart: 11 -> 19, of which waited for: 2 -> 8; matrix products, arithmetic and copies ran while one was open for 9% -> 7% of each run, Pallas kernels for 16% -> 17%
where the time goes in v3:
time: 208 us; the launch traced here: 207 us
  waiting for transfers between devices  76.4 us (37%)
  Pallas kernels  51.6 us (25%)
  starting transfers between devices  43 us (21%)
  local copies, waits for them, and re-layouts  17.7 us (9%)
  between operations  13.9 us (7%)
  other arithmetic  4.11 us (2%)
    ppermute x7, waiting for transfers between devices, to(): return lax.ppermute(a, 'fsdp', pairs)  39.4 us
    ppermute x8, waiting for transfers between devices, to(): return lax.ppermute(a, 'section', pairs)  32 us
    pallas_call x1, Pallas kernels, look(): pl.pallas_call(functools.partial(look_kernel, quarter), out_shape=jax.Sha...  21.6 us
    ppermute x7, starting transfers between devices, to(): return lax.ppermute(a, 'fsdp', pairs)  15.5 us
    pallas_call x1, Pallas kernels, mix(): pl.pallas_call(functools.partial(mix_kernel, len(pieces)), out_shape=[sha...  15 us
    ppermute x8, starting transfers between devices, to(): return lax.ppermute(a, 'section', pairs)  10.9 us
    unnamed x13, local copies, waits for them, and re-layouts  9.91 us
    pallas_call x1, Pallas kernels, turn(): pl.pallas_call(turn_kernel, out_shape=jax.ShapeDtypeStruct((quarter, LANE...  7.28 us
  transfers between devices with their start and end apart: 19, of which 8 were waited for; matrix products, arithmetic and copies ran while one was open for 7% of the time, Pallas kernels for 17%

profile of v3, /device:TPU:2, one launch (start us, length us, event | category | flops | bytes accessed | tf_op | source)
XLA Modules:
  0.0 206.7 jit_solution(5033937748364189977)
XLA Ops:
  6.5 1.8 pad_maximum_fusion.1
  10.0 3.3 %collective-permute-start = (bf16[16,4096]{1,0:T(8,128)(2,1)S(1)}, bf16[16,4096]{1,0:T(8,128)(2,1)S(1)}, u32[]{:S(2)}, u32[]{:S(2)}) collective-permute-start(bf16[16,4096]{1,0:T(8,128)(2,1)S(1)} %get-tuple-element.31), channel_id=1, source_target_pairs={{0,8},{1,9},{2,10},{3,11},{4,12},{5,13},{6,14},{7,15},{8,16},{9,17... | collective-permute-start | bytes 393224 | tf_op jit(solution)/shard_map/ppermute | solution.py:251
  13.2 3.0 %collective-permute-start.1 = (bf16[16,4096]{1,0:T(8,128)(2,1)S(1)}, bf16[16,4096]{1,0:T(8,128)(2,1)S(1)}, u32[]{:S(2)}, u32[]{:S(2)}) collective-permute-start(bf16[16,4096]{1,0:T(8,128)(2,1)S(1)} %get-tuple-element.31), channel_id=1, source_target_pairs={{0,24},{1,25},{2,26},{3,27},{4,28},{5,29},{6,30},{7,31},{8,0},{9,1... | collective-permute-start | bytes 393224 | tf_op jit(solution)/shard_map/ppermute | solution.py:251
  16.3 5.0 %collective-permute-start.2 = (bf16[16,4096]{1,0:T(8,128)(2,1)S(1)}, bf16[16,4096]{1,0:T(8,128)(2,1)S(1)}, u32[]{:S(2)}, u32[]{:S(2)}) collective-permute-start(bf16[16,4096]{1,0:T(8,128)(2,1)S(1)} %get-tuple-element.31), channel_id=1, source_target_pairs={{0,16},{1,17},{2,18},{3,19},{4,20},{5,21},{6,22},{7,23},{8,24},{9,... | collective-permute-start | bytes 393224 | tf_op jit(solution)/shard_map/ppermute | solution.py:251
  22.7 5.3 %all-to-all-start = ((s32[32,1,512]{2,1,0:T(1,128)}), s32[32,1,512]{2,1,0:T(1,128)S(1)}, u32[]{:S(2)}, u32[]{:S(2)}) async-start(s32[32,1,512]{2,1,0:T(1,128)} %broadcast_in_dim.67), calls=%async_computation | async-start | bytes 131072 | tf_op jit(solution)/shard_map/all_to_all | solution.py:278
  28.7 7.3 %turn.1 = f32[16384,128]{1,0:T(8,128)} custom-call(bf16[28,65536]{1,0:T(8,128)(2,1)} %refs_3_.1, bf16[28,65536]{1,0:T(8,128)(2,1)} %refs_3_.1, bf16[28,65536]{1,0:T(8,128)(2,1)} %refs_3_.1, bf16[28,65536]{1,0:T(8,128)(2,1)} %refs_3_.1), custom_call_target="tpu_custom_call" | custom-call | tf_op jit(solution)/shard_map/turn/pallas_call | solution.py:39
  36.0 2.8 %all-to-all-done = s32[32,1,512]{2,1,0:T(1,128)S(1)} async-done(((s32[32,1,512]{2,1,0:T(1,128)}), s32[32,1,512]{2,1,0:T(1,128)S(1)}, u32[]{:S(2)}, u32[]{:S(2)}) %all-to-all-start) | async-done | bytes 65568 | tf_op jit(solution)/shard_map/all_to_all | solution.py:278
  40.6 3.4 %copy-done = f32[16384,128]{1,0:T(8,128)S(1)} copy-done((f32[16384,128]{1,0:T(8,128)S(1)}, f32[16384,128]{1,0:T(8,128)}, u32[]{:S(2)}) %copy-start) | copy-done | bytes 8388632
  44.0 21.6 %look.1 = bf16[32,32,512]{2,1,0:T(8,128)(2,1)} custom-call(s32[32,1,512]{2,1,0:T(1,128)S(1)} %and_select_fusion.1.row_ref, s32[32,1,512]{2,1,0:T(1,128)S(1)} %get-tuple-element.29.grp_ref, f32[16384,1,128]{2,1,0:T(1,128)S(1)} %bitcast.53), custom_call_target="tpu_custom_call" | custom-call | tf_op jit(solution)/shard_map/look/pallas_call | solution.py:73
  65.6 7.0 %all-to-all-start.1 = ((bf16[32,32,512]{2,1,0:T(8,128)(2,1)}), bf16[32,32,512]{2,1,0:T(8,128)(2,1)S(1)}, u32[]{:S(2)}, u32[]{:S(2)}) async-start(bf16[32,32,512]{2,1,0:T(8,128)(2,1)} %look.1), calls=%async_computation.1 | async-start | bytes 2097152 | tf_op jit(solution)/shard_map/all_to_all | solution.py:287
  74.8 2.1 %collective-permute-start.5 = (bf16[64,4096]{1,0:T(8,128)(2,1)S(1)}, bf16[64,4096]{1,0:T(8,128)(2,1)S(1)}, u32[]{:S(2)}, u32[]{:S(2)}) collective-permute-start(bf16[64,4096]{1,0:T(8,128)(2,1)S(1)} %pad_maximum_fusion), channel_id=1, source_target_pairs={{0,4},{1,5},{2,6},{3,7},{4,0},{5,1},{6,2},{7,3},{8,12},{9,13},{10,... | collective-permute-start | bytes 1572872 | tf_op jit(solution)/shard_map/ppermute | solution.py:251
  78.8 26.3 %collective-permute-done.3 = bf16[64,4096]{1,0:T(8,128)(2,1)S(1)} collective-permute-done((bf16[64,4096]{1,0:T(8,128)(2,1)S(1)}, bf16[64,4096]{1,0:T(8,128)(2,1)S(1)}, u32[]{:S(2)}, u32[]{:S(2)}) %collective-permute-start.3) | collective-permute-done | bytes 524320 | tf_op jit(solution)/shard_map/ppermute | solution.py:251
  106.8 13.1 %collective-permute-done.5 = bf16[64,4096]{1,0:T(8,128)(2,1)S(1)} collective-permute-done((bf16[64,4096]{1,0:T(8,128)(2,1)S(1)}, bf16[64,4096]{1,0:T(8,128)(2,1)S(1)}, u32[]{:S(2)}, u32[]{:S(2)}) %collective-permute-start.5) | collective-permute-done | bytes 524320 | tf_op jit(solution)/shard_map/ppermute | solution.py:251
  123.9 2.2 %all-to-all-done.1.e_ref = bf16[32,32,512]{2,1,0:T(8,128)(2,1)S(1)} async-done(((bf16[32,32,512]{2,1,0:T(8,128)(2,1)}), bf16[32,32,512]{2,1,0:T(8,128)(2,1)S(1)}, u32[]{:S(2)}, u32[]{:S(2)}) %all-to-all-start.1) | async-done | bytes 1048608 | tf_op jit(solution)/shard_map/all_to_all | solution.py:287
  127.0 4.3 %all-to-all-start.2 = ((f32[8,2,512]{2,1,0:T(2,128)}), f32[8,2,512]{2,1,0:T(2,128)S(1)}, u32[]{:S(2)}, u32[]{:S(2)}) async-start(f32[8,2,512]{2,1,0:T(2,128)} %broadcast_in_dim.77), calls=%async_computation.2 | async-start | bytes 65536 | tf_op jit(solution)/shard_map/all_to_all | solution.py:305
  131.3 5.4 %prep.1.refs_0_ = bf16[512,1792]{1,0:T(8,128)(2,1)S(1)} custom-call(bf16[512,896]{1,0:T(8,128)(2,1)S(1)} %copy-done.2, bf16[32,32,512]{2,1,0:T(8,128)(2,1)S(1)} %all-to-all-done.1.e_ref, s32[1,1792]{1,0:T(1,128)S(1)} %broadcast_in_dim.72.s_ref), custom_call_target="tpu_custom_call" | custom-call | flops 3523215360 | bytes 8388608 | tf_op jit(solution)/shard_map/prep/pallas_call | solution.py:112
  138.0 15.0 %mix.1 = (bf16[4,512,256]{2,1,0:T(8,128)(2,1)S(1)}, f32[4,512,256]{2,1,0:T(8,128)}, bf16[2,512,256]{2,1,0:T(8,128)(2,1)S(1)}, bf16[2,512,256]{2,1,0:T(8,128)(2,1...) custom-call(s32[8]{0:T(128)S(1)} %stack.143.order_ref, bf16[512,1792]{1,0:T(8,128)(2,1)} %copy-done.3, ...), custom_call_target="tpu_custom_call" | custom-call | flops 7516192768 | bytes 29360128 | tf_op jit(solution)/shard_map/mix/pallas_call | solution.py:173
  153.1 2.0 collective-permute-start.7
  155.1 2.7 %collective-permute-start.10 = (bf16[2,512,256]{2,1,0:T(8,128)(2,1)S(1)}, bf16[2,512,256]{2,1,0:T(8,128)(2,1)S(1)}, u32[]{:S(2)}, u32[]{:S(2)}) collective-permute-start(bf16[2,512,256]{2,1,0:T(8,128)(2,1)S(1)} %get-tuple-element.22), channel_id=1, source_target_pairs={{0,96},{32,0},{64,32},{96,64},{128,224},{160,128},{192,160},{224,1... | collective-permute-start | bytes 1572872 | tf_op jit(solution)/shard_map/ppermute | solution.py:213
  157.8 2.3 %collective-permute-start.9 = (bf16[2,512,256]{2,1,0:T(8,128)(2,1)S(1)}, bf16[2,512,256]{2,1,0:T(8,128)(2,1)S(1)}, u32[]{:S(2)}, u32[]{:S(2)}) collective-permute-start(bf16[2,512,256]{2,1,0:T(8,128)(2,1)S(1)} %get-tuple-element.21), channel_id=1, source_target_pairs={{0,64},{32,96},{64,0},{96,32},{128,192},{160,224},{192,128},{224,1... | collective-permute-start | bytes 1572872 | tf_op jit(solution)/shard_map/ppermute | solution.py:213
  160.1 19.5 %collective-permute-done.10.b_3 = bf16[2,512,256]{2,1,0:T(8,128)(2,1)S(1)} collective-permute-done((bf16[2,512,256]{2,1,0:T(8,128)(2,1)S(1)}, bf16[2,512,256]{2,1,0:T(8,128)(2,1)S(1)}, u32[]{:S(2)}, u32[]{:S(2)}) %collective-permute-start.10) | collective-permute-done | bytes 524320 | tf_op jit(solution)/shard_map/ppermute | solution.py:213
  179.6 3.4 %collective-permute-done.8.b_1 = bf16[2,512,256]{2,1,0:T(8,128)(2,1)S(1)} collective-permute-done((bf16[2,512,256]{2,1,0:T(8,128)(2,1)S(1)}, bf16[2,512,256]{2,1,0:T(8,128)(2,1)S(1)}, u32[]{:S(2)}, u32[]{:S(2)}) %collective-permute-start.8) | collective-permute-done | bytes 524320 | tf_op jit(solution)/shard_map/ppermute | solution.py:213
  185.6 1.7 collective-permute-start.12
  189.4 8.4 %collective-permute-done.11.a_1 = bf16[512,256]{1,0:T(8,128)(2,1)S(1)} collective-permute-done((bf16[512,256]{1,0:T(8,128)(2,1)S(1)}, bf16[512,256]{1,0:T(8,128)(2,1)S(1)}, u32[]{:S(2)}, u32[]{:S(2)}) %collective-permute-start.11) | collective-permute-done | bytes 262176 | tf_op jit(solution)/shard_map/ppermute | solution.py:213
  (82 shorter events, 23.9 us)
Async XLA Ops:
  6.5 131.5 %all-gather.2.cloned.1.call-start = ((), (), s32[]{:S(2)}) async-start(), calls=%async_computation.3 | async-start | bytes 10813440 | tf_op jit(solution)/shard_map/all_gather | solution.py:281
  10.0 62.6 %collective-permute-start = (bf16[16,4096]{1,0:T(8,128)(2,1)S(1)}, bf16[16,4096]{1,0:T(8,128)(2,1)S(1)}, u32[]{:S(2)}, u32[]{:S(2)}) collective-permute-start(bf16[16,4096]{1,0:T(8,128)(2,1)S(1)} %get-tuple-element.31), channel_id=1, source_target_pairs={{0,8},{1,9},{2,10},{3,11},{4,12},{5,13},{6,14},{7,15},{8,16},{9,17... | collective-permute-start | bytes 393224 | tf_op jit(solution)/shard_map/ppermute | solution.py:251
  13.2 59.4 %collective-permute-start.1 = (bf16[16,4096]{1,0:T(8,128)(2,1)S(1)}, bf16[16,4096]{1,0:T(8,128)(2,1)S(1)}, u32[]{:S(2)}, u32[]{:S(2)}) collective-permute-start(bf16[16,4096]{1,0:T(8,128)(2,1)S(1)} %get-tuple-element.31), channel_id=1, source_target_pairs={{0,24},{1,25},{2,26},{3,27},{4,28},{5,29},{6,30},{7,31},{8,0},{9,1... | collective-permute-start | bytes 393224 | tf_op jit(solution)/shard_map/ppermute | solution.py:251
  16.3 56.4 %collective-permute-start.2 = (bf16[16,4096]{1,0:T(8,128)(2,1)S(1)}, bf16[16,4096]{1,0:T(8,128)(2,1)S(1)}, u32[]{:S(2)}, u32[]{:S(2)}) collective-permute-start(bf16[16,4096]{1,0:T(8,128)(2,1)S(1)} %get-tuple-element.31), channel_id=1, source_target_pairs={{0,16},{1,17},{2,18},{3,19},{4,20},{5,21},{6,22},{7,23},{8,24},{9,... | collective-permute-start | bytes 393224 | tf_op jit(solution)/shard_map/ppermute | solution.py:251
  22.7 16.1 %all-to-all-start = ((s32[32,1,512]{2,1,0:T(1,128)}), s32[32,1,512]{2,1,0:T(1,128)S(1)}, u32[]{:S(2)}, u32[]{:S(2)}) async-start(s32[32,1,512]{2,1,0:T(1,128)} %broadcast_in_dim.67), calls=%async_computation | async-start | bytes 131072 | tf_op jit(solution)/shard_map/all_to_all | solution.py:278
  40.5 3.4 %copy-start = (f32[16384,128]{1,0:T(8,128)S(1)}, f32[16384,128]{1,0:T(8,128)}, u32[]{:S(2)}) copy-start(f32[16384,128]{1,0:T(8,128)} %turn.1) | copy-start | bytes 25165828
  65.6 60.5 %all-to-all-start.1 = ((bf16[32,32,512]{2,1,0:T(8,128)(2,1)}), bf16[32,32,512]{2,1,0:T(8,128)(2,1)S(1)}, u32[]{:S(2)}, u32[]{:S(2)}) async-start(bf16[32,32,512]{2,1,0:T(8,128)(2,1)} %look.1), calls=%async_computation.1 | async-start | bytes 2097152 | tf_op jit(solution)/shard_map/all_to_all | solution.py:287
  72.7 32.4 %collective-permute-start.3 = (bf16[64,4096]{1,0:T(8,128)(2,1)S(1)}, bf16[64,4096]{1,0:T(8,128)(2,1)S(1)}, u32[]{:S(2)}, u32[]{:S(2)}) collective-permute-start(bf16[64,4096]{1,0:T(8,128)(2,1)S(1)} %pad_maximum_fusion), channel_id=1, source_target_pairs={{0,2},{1,3},{2,4},{3,5},{4,6},{5,7},{6,0},{7,1},{8,10},{9,11},{10,... | collective-permute-start | bytes 1572872 | tf_op jit(solution)/shard_map/ppermute | solution.py:251
  74.2 31.7 %collective-permute-start.4 = (bf16[64,4096]{1,0:T(8,128)(2,1)S(1)}, bf16[64,4096]{1,0:T(8,128)(2,1)S(1)}, u32[]{:S(2)}, u32[]{:S(2)}) collective-permute-start(bf16[64,4096]{1,0:T(8,128)(2,1)S(1)} %pad_maximum_fusion), channel_id=1, source_target_pairs={{0,6},{1,7},{2,0},{3,1},{4,2},{5,3},{6,4},{7,5},{8,14},{9,15},{10,... | collective-permute-start | bytes 1572872 | tf_op jit(solution)/shard_map/ppermute | solution.py:251
  74.8 45.1 %collective-permute-start.5 = (bf16[64,4096]{1,0:T(8,128)(2,1)S(1)}, bf16[64,4096]{1,0:T(8,128)(2,1)S(1)}, u32[]{:S(2)}, u32[]{:S(2)}) collective-permute-start(bf16[64,4096]{1,0:T(8,128)(2,1)S(1)} %pad_maximum_fusion), channel_id=1, source_target_pairs={{0,4},{1,5},{2,6},{3,7},{4,0},{5,1},{6,2},{7,3},{8,12},{9,13},{10,... | collective-permute-start | bytes 1572872 | tf_op jit(solution)/shard_map/ppermute | solution.py:251
  77.5 46.1 %copy-start.2 = (bf16[512,896]{1,0:T(8,128)(2,1)S(1)}, bf16[512,896]{1,0:T(8,128)(2,1)}, u32[]{:S(2)}) copy-start(bf16[512,896]{1,0:T(8,128)(2,1)} %h_ref.1) | copy-start | bytes 2752516
  120.7 17.3 %collective-permute-start.6 = (bf16[256,4096]{1,0:T(8,128)(2,1)}, bf16[256,4096]{1,0:T(8,128)(2,1)}, u32[]{:S(2)}, u32[]{:S(2)}) collective-permute-start(bf16[256,4096]{1,0:T(8,128)(2,1)} %constant_dynamic-update-slice_fusion.refs_5_), channel_id=1, source_target_pairs={{0,1},{1,0},{2,3},{3,2},{4,5},{5,4},{6,7},{7,6},{8,9},{9,8},{10,11... | collective-permute-start | bytes 6291464 | tf_op jit(solution)/shard_map/ppermute | solution.py:251
  127.0 10.9 %all-to-all-start.2 = ((f32[8,2,512]{2,1,0:T(2,128)}), f32[8,2,512]{2,1,0:T(2,128)S(1)}, u32[]{:S(2)}, u32[]{:S(2)}) async-start(f32[8,2,512]{2,1,0:T(2,128)} %broadcast_in_dim.77), calls=%async_computation.2 | async-start | bytes 65536 | tf_op jit(solution)/shard_map/all_to_all | solution.py:305
  136.7 1.2 copy-start.3
  153.1 29.9 %collective-permute-start.7 = (bf16[4,512,256]{2,1,0:T(8,128)(2,1)S(1)}, bf16[4,512,256]{2,1,0:T(8,128)(2,1)S(1)}, u32[]{:S(2)}, u32[]{:S(2)}) collective-permute-start(bf16[4,512,256]{2,1,0:T(8,128)(2,1)S(1)} %get-tuple-element.18), channel_id=1, source_target_pairs={{0,128},{32,160},{64,192},{96,224},{128,0},{160,32},{192,64},{224,... | collective-permute-start | bytes 3145736 | tf_op jit(solution)/shard_map/ppermute | solution.py:213
  155.1 24.5 %collective-permute-start.10 = (bf16[2,512,256]{2,1,0:T(8,128)(2,1)S(1)}, bf16[2,512,256]{2,1,0:T(8,128)(2,1)S(1)}, u32[]{:S(2)}, u32[]{:S(2)}) collective-permute-start(bf16[2,512,256]{2,1,0:T(8,128)(2,1)S(1)} %get-tuple-element.22), channel_id=1, source_target_pairs={{0,96},{32,0},{64,32},{96,64},{128,224},{160,128},{192,160},{224,1... | collective-permute-start | bytes 1572872 | tf_op jit(solution)/shard_map/ppermute | solution.py:213
  157.8 25.2 %collective-permute-start.8 = (bf16[2,512,256]{2,1,0:T(8,128)(2,1)S(1)}, bf16[2,512,256]{2,1,0:T(8,128)(2,1)S(1)}, u32[]{:S(2)}, u32[]{:S(2)}) collective-permute-start(bf16[2,512,256]{2,1,0:T(8,128)(2,1)S(1)} %get-tuple-element.20), channel_id=1, source_target_pairs={{0,32},{32,64},{64,96},{96,0},{128,160},{160,192},{192,224},{224,1... | collective-permute-start | bytes 1572872 | tf_op jit(solution)/shard_map/ppermute | solution.py:213
  157.8 25.2 %collective-permute-start.9 = (bf16[2,512,256]{2,1,0:T(8,128)(2,1)S(1)}, bf16[2,512,256]{2,1,0:T(8,128)(2,1)S(1)}, u32[]{:S(2)}, u32[]{:S(2)}) collective-permute-start(bf16[2,512,256]{2,1,0:T(8,128)(2,1)S(1)} %get-tuple-element.21), channel_id=1, source_target_pairs={{0,64},{32,96},{64,0},{96,32},{128,192},{160,224},{192,128},{224,1... | collective-permute-start | bytes 1572872 | tf_op jit(solution)/shard_map/ppermute | solution.py:213
  183.0 1.6 copy-start.1
  185.5 12.3 %collective-permute-start.11 = (bf16[512,256]{1,0:T(8,128)(2,1)S(1)}, bf16[512,256]{1,0:T(8,128)(2,1)S(1)}, u32[]{:S(2)}, u32[]{:S(2)}) collective-permute-start(bf16[512,256]{1,0:T(8,128)(2,1)S(1)} %get-tuple-element.24), channel_id=1, source_target_pairs={{0,32},{32,64},{64,96},{96,0},{128,160},{160,192},{192,224},{224,1... | collective-permute-start | bytes 786440 | tf_op jit(solution)/shard_map/ppermute | solution.py:213
  185.6 12.2 %collective-permute-start.12 = (bf16[512,256]{1,0:T(8,128)(2,1)S(1)}, bf16[512,256]{1,0:T(8,128)(2,1)S(1)}, u32[]{:S(2)}, u32[]{:S(2)}) collective-permute-start(bf16[512,256]{1,0:T(8,128)(2,1)S(1)} %get-tuple-element.25), channel_id=1, source_target_pairs={{0,64},{32,96},{64,0},{96,32},{128,192},{160,224},{192,128},{224,1... | collective-permute-start | bytes 786440 | tf_op jit(solution)/shard_map/ppermute | solution.py:213
  187.3 11.1 %collective-permute-start.13 = (bf16[512,256]{1,0:T(8,128)(2,1)S(1)}, bf16[512,256]{1,0:T(8,128)(2,1)S(1)}, u32[]{:S(2)}, u32[]{:S(2)}) collective-permute-start(bf16[512,256]{1,0:T(8,128)(2,1)S(1)} %get-tuple-element.26), channel_id=1, source_target_pairs={{0,96},{32,0},{64,32},{96,64},{128,224},{160,128},{192,160},{224,1... | collective-permute-start | bytes 786440 | tf_op jit(solution)/shard_map/ppermute | solution.py:213
  188.8 9.6 %collective-permute-start.14 = (bf16[512,256]{1,0:T(8,128)(2,1)S(1)}, bf16[512,256]{1,0:T(8,128)(2,1)S(1)}, u32[]{:S(2)}, u32[]{:S(2)}) collective-permute-start(bf16[512,256]{1,0:T(8,128)(2,1)S(1)} %get-tuple-element.28), channel_id=1, source_target_pairs={{0,128},{32,160},{64,192},{96,224},{128,0},{160,32},{192,64},{224,... | collective-permute-start | bytes 786440 | tf_op jit(solution)/shard_map/ppermute | solution.py:213
Sparse Core Ops, SparseCore 0:
  9.9 110.1 all-gather.1

commit v4 on v3

--- a/solution.py
+++ b/solution.py
@@ -119,12 +119,21 @@
     )(h, e, source)
 
 
-def mix_kernel(n_pieces, order_ref, *refs):
+def product(left_ref, pieces):
+    at, acc = 0, None
+    for p in pieces:
+        rows = p.shape[0]
+        term = jnp.dot(left_ref[:, at : at + rows], p[...], preferred_element_type=f32)
+        acc = term if acc is None else acc + term
+        at += rows
+    return acc
+
+
+def send_kernel(n_pieces, order_ref, *refs):
     x_ref, g_ref, m_ref, s_ref = refs[:4]
     pieces = refs[4 : 4 + n_pieces]
-    a_send, a_keep, b_1, b_2, b_3, b_keep, left_ref = refs[4 + n_pieces :]
+    a_send, b_1, b_2, b_3, left_ref = refs[4 + n_pieces :]
     n = pl.program_id(0)
-    side = n % 4
 
     @pl.when(n == 0)
     def _():
@@ -136,58 +145,72 @@
             scale = jnp.where(m_ref[:, at] > 0, scale_h, scale_e)
             left_ref[:, at] = (x_ref[:, at].astype(f32) * scale * g_ref[:, at]).astype(bf)
 
-    at, acc = 0, None
-    for p in pieces:
-        rows = p.shape[0]
-        term = jnp.dot(left_ref[:, at : at + rows], p[...], preferred_element_type=f32)
-        acc = term if acc is None else acc + term
-        at += rows
-    half = acc.shape[1] // 2
+    value = product(left_ref, pieces).astype(bf)
+    for ref, first, end in ((a_send, 0, 4), (b_1, 4, 6), (b_2, 6, 8), (b_3, 8, 10)):
+
+        @pl.when((n >= first) & (n < end))
+        def _():
+            ref[0] = value
+
+
+def keep_kernel(n_pieces, order_ref, left_ref, *refs):
+    pieces = refs[:n_pieces]
+    a_keep, b_keep = refs[n_pieces:]
+    n = pl.program_id(0)
+    value = product(left_ref, pieces)
 
     @pl.when(n < 4)
     def _():
-        a_send[0] = acc[:, :half].astype(bf)
+        a_keep[0] = value
 
     @pl.when(n >= 4)
     def _():
-        a_keep[0] = acc[:, :half]
-
-    for i, ref in enumerate((b_1, b_2, b_3, b_keep)):
-
-        @pl.when(side == i)
-        def _():
-            ref[0] = acc[:, half:].astype(ref.dtype)
+        b_keep[0] = value
 
 
 def mix(x, gain, is_hidden, scales, pieces, sections):
     tokens, depth = x.shape
-    cols = pieces[0].shape[1] // sections
-    half = cols // 2
+    half = pieces[0].shape[1] // sections // 2
     section = lax.axis_index("section")
     z, y = section // 4, section % 4
-    order = jnp.stack([(zz * 4 + (y + 1 + i) % 4) for zz in (1 - z, z) for i in range(4)])
+    place = lambda zz, d, part: (zz * 4 + (y + d) % 4) * 2 + part
+    out_order = [place(1 - z, d, 0) for d in (1, 2, 3, 0)] + [place(zz, d, 1) for d in (1, 2, 3) for zz in (1 - z, z)]
+    own_order = [place(z, d, 0) for d in (1, 2, 3, 0)] + [place(zz, 0, 1) for zz in (1 - z, z)]
     whole = lambda n, order: (0, 0)
-    block = lambda place: pl.BlockSpec((1, tokens, half), lambda n, order: (place(n), 0, 0))
+    columns = [pl.BlockSpec((p.shape[0], half), lambda n, order: (0, order[n])) for p in pieces]
+    block = lambda first, count: pl.BlockSpec((1, tokens, half), lambda n, order: (jnp.clip(n - first, 0, count - 1), 0, 0))
     shape = lambda count, kind: jax.ShapeDtypeStruct((count, tokens, half), kind)
-    later = lambda i: lambda n: jnp.where(n < 4 + i, 0, 1)
-    return pl.pallas_call(
-        functools.partial(mix_kernel, len(pieces)),
-        out_shape=[shape(4, bf), shape(4, f32), shape(2, bf), shape(2, bf), shape(2, bf), shape(2, f32)],
+    params = pltpu.CompilerParams(vmem_limit_bytes=50 << 20)
+    cost = lambda steps: pl.CostEstimate(
+        flops=2 * tokens * depth * half * steps, bytes_accessed=4 * depth * half * steps, transcendentals=0
+    )
+    a_send, b_1, b_2, b_3, left = pl.pallas_call(
+        functools.partial(send_kernel, len(pieces)),
+        out_shape=[shape(4, bf), shape(2, bf), shape(2, bf), shape(2, bf), jax.ShapeDtypeStruct((tokens, depth), bf)],
         grid_spec=pltpu.PrefetchScalarGridSpec(
             num_scalar_prefetch=1,
-            grid=(sections,),
-            in_specs=[pl.BlockSpec(a.shape, whole) for a in (x, gain, is_hidden, scales)]
-            + [pl.BlockSpec((p.shape[0], cols), lambda n, order: (0, order[n])) for p in pieces],
-            out_specs=[block(lambda n: jnp.minimum(n, 3)), block(lambda n: jnp.maximum(n - 4, 0))]
-            + [block(later(i)) for i in range(4)],
-            scratch_shapes=[pltpu.VMEM((tokens, depth), bf)],
+            grid=(len(out_order),),
+            in_specs=[pl.BlockSpec(v.shape, whole) for v in (x, gain, is_hidden, scales)] + columns,
+            out_specs=[block(0, 4), block(4, 2), block(6, 2), block(8, 2), pl.BlockSpec((tokens, depth), whole)],
         ),
-        compiler_params=pltpu.CompilerParams(vmem_limit_bytes=50 << 20),
-        cost_estimate=pl.CostEstimate(
-            flops=2 * tokens * depth * cols * sections, bytes_accessed=4 * depth * cols * sections, transcendentals=0
+        compiler_params=params,
+        cost_estimate=cost(len(out_order)),
+        name="mix_sent",
+    )(jnp.stack(out_order), x, gain, is_hidden, scales, *pieces)
+    a_keep, b_keep = pl.pallas_call(
+        functools.partial(keep_kernel, len(pieces)),
+        out_shape=[shape(4, f32), shape(2, f32)],
+        grid_spec=pltpu.PrefetchScalarGridSpec(
+            num_scalar_prefetch=1,
+            grid=(len(own_order),),
+            in_specs=[pl.BlockSpec((tokens, depth), whole)] + columns,
+            out_specs=[block(0, 4), block(4, 2)],
         ),
-        name="mix",
-    )(order, x, gain, is_hidden, scales, *pieces)
+        compiler_params=params,
+        cost_estimate=cost(len(own_order)),
+        name="mix_kept",
+    )(jnp.stack(own_order), left, *pieces)
+    return a_send, a_keep, b_1, b_2, b_3, b_keep
 
 
 def fold_kernel(a_keep, a_in, b_keep, b_1, b_2, b_3, a_1, a_2, a_3, a_own, b_send, b_own):

time: 208 us -> 207 us (level)
  waiting for transfers between devices: 76.4 us -> 67.1 us
  Pallas kernels: 51.6 us -> 58.7 us
    ppermute x8, waiting for transfers between devices: 32 us -> 22.5 us  [to(): return lax.ppermute(a, 'section', pairs)]
    pallas_call x1 -> x2, Pallas kernels: 15 us -> 22.1 us  [the longest x1 14 us: mix(): pl.pallas_call(functools.partial(send_kernel, len(pieces)), out_shape=[sh...]
    unnamed x13 -> x15, local copies, waits for them, and re-layouts: 9.91 us -> 11.4 us
  transfers between devices with their start and end apart: 19 -> 19, of which waited for: 8 -> 8; matrix products, arithmetic and copies ran while one was open for 7% -> 7% of each run, Pallas kernels for 17% -> 21%
where the time goes in v4:
time: 207 us; the launch traced here: 206 us
  waiting for transfers between devices  67.1 us (32%)
  Pallas kernels  58.7 us (28%)
  starting transfers between devices  43.1 us (21%)
  local copies, waits for them, and re-layouts  19.1 us (9%)
  between operations  13.9 us (7%)
  other arithmetic  3.98 us (2%)
    ppermute x7, waiting for transfers between devices, to(): return lax.ppermute(a, 'fsdp', pairs)  39.5 us
    ppermute x8, waiting for transfers between devices, to(): return lax.ppermute(a, 'section', pairs)  22.5 us
    pallas_call x1, Pallas kernels, look(): pl.pallas_call(functools.partial(look_kernel, quarter), out_shape=jax.Sha...  21.6 us
    ppermute x7, starting transfers between devices, to(): return lax.ppermute(a, 'fsdp', pairs)  15.5 us
    pallas_call x1, Pallas kernels, mix(): pl.pallas_call(functools.partial(send_kernel, len(pieces)), out_shape=[sh...  14 us
    unnamed x15, local copies, waits for them, and re-layouts  11.4 us
    ppermute x8, starting transfers between devices, to(): return lax.ppermute(a, 'section', pairs)  11 us
    pallas_call x1, Pallas kernels, mix(): pl.pallas_call(functools.partial(keep_kernel, len(pieces)), out_shape=[sh...  8.06 us
  transfers between devices with their start and end apart: 19, of which 8 were waited for; matrix products, arithmetic and copies ran while one was open for 7% of the time, Pallas kernels for 21%

profile of v4, /device:TPU:2, one launch (start us, length us, event | category | flops | bytes accessed | tf_op | source)
XLA Modules:
  0.0 205.9 jit_solution(6097147647952965314)
XLA Ops:
  6.5 1.8 pad_maximum_fusion.1
  10.0 3.3 %collective-permute-start = (bf16[16,4096]{1,0:T(8,128)(2,1)S(1)}, bf16[16,4096]{1,0:T(8,128)(2,1)S(1)}, u32[]{:S(2)}, u32[]{:S(2)}) collective-permute-start(bf16[16,4096]{1,0:T(8,128)(2,1)S(1)} %get-tuple-element.33), channel_id=1, source_target_pairs={{0,8},{1,9},{2,10},{3,11},{4,12},{5,13},{6,14},{7,15},{8,16},{9,17... | collective-permute-start | bytes 393224 | tf_op jit(solution)/shard_map/ppermute | solution.py:274
  13.3 3.0 %collective-permute-start.1 = (bf16[16,4096]{1,0:T(8,128)(2,1)S(1)}, bf16[16,4096]{1,0:T(8,128)(2,1)S(1)}, u32[]{:S(2)}, u32[]{:S(2)}) collective-permute-start(bf16[16,4096]{1,0:T(8,128)(2,1)S(1)} %get-tuple-element.33), channel_id=1, source_target_pairs={{0,24},{1,25},{2,26},{3,27},{4,28},{5,29},{6,30},{7,31},{8,0},{9,1... | collective-permute-start | bytes 393224 | tf_op jit(solution)/shard_map/ppermute | solution.py:274
  16.3 5.0 %collective-permute-start.2 = (bf16[16,4096]{1,0:T(8,128)(2,1)S(1)}, bf16[16,4096]{1,0:T(8,128)(2,1)S(1)}, u32[]{:S(2)}, u32[]{:S(2)}) collective-permute-start(bf16[16,4096]{1,0:T(8,128)(2,1)S(1)} %get-tuple-element.33), channel_id=1, source_target_pairs={{0,16},{1,17},{2,18},{3,19},{4,20},{5,21},{6,22},{7,23},{8,24},{9,... | collective-permute-start | bytes 393224 | tf_op jit(solution)/shard_map/ppermute | solution.py:274
  22.6 5.3 %all-to-all-start = ((s32[32,1,512]{2,1,0:T(1,128)}), s32[32,1,512]{2,1,0:T(1,128)S(1)}, u32[]{:S(2)}, u32[]{:S(2)}) async-start(s32[32,1,512]{2,1,0:T(1,128)} %broadcast_in_dim.67), calls=%async_computation | async-start | bytes 131072 | tf_op jit(solution)/shard_map/all_to_all | solution.py:301
  28.7 7.3 %turn.1 = f32[16384,128]{1,0:T(8,128)} custom-call(bf16[28,65536]{1,0:T(8,128)(2,1)} %refs_3_.1, bf16[28,65536]{1,0:T(8,128)(2,1)} %refs_3_.1, bf16[28,65536]{1,0:T(8,128)(2,1)} %refs_3_.1, bf16[28,65536]{1,0:T(8,128)(2,1)} %refs_3_.1), custom_call_target="tpu_custom_call" | custom-call | tf_op jit(solution)/shard_map/turn/pallas_call | solution.py:39
  36.0 2.8 %all-to-all-done = s32[32,1,512]{2,1,0:T(1,128)S(1)} async-done(((s32[32,1,512]{2,1,0:T(1,128)}), s32[32,1,512]{2,1,0:T(1,128)S(1)}, u32[]{:S(2)}, u32[]{:S(2)}) %all-to-all-start) | async-done | bytes 65568 | tf_op jit(solution)/shard_map/all_to_all | solution.py:301
  40.3 3.4 %copy-done = f32[16384,128]{1,0:T(8,128)S(1)} copy-done((f32[16384,128]{1,0:T(8,128)S(1)}, f32[16384,128]{1,0:T(8,128)}, u32[]{:S(2)}) %copy-start) | copy-done | bytes 8388632
  43.8 21.6 %look.1 = bf16[32,32,512]{2,1,0:T(8,128)(2,1)} custom-call(s32[32,1,512]{2,1,0:T(1,128)S(1)} %and_select_fusion.1.row_ref, s32[32,1,512]{2,1,0:T(1,128)S(1)} %get-tuple-element.31.grp_ref, f32[16384,1,128]{2,1,0:T(1,128)S(1)} %bitcast.61), custom_call_target="tpu_custom_call" | custom-call | tf_op jit(solution)/shard_map/look/pallas_call | solution.py:73
  65.4 7.0 %all-to-all-start.1 = ((bf16[32,32,512]{2,1,0:T(8,128)(2,1)}), bf16[32,32,512]{2,1,0:T(8,128)(2,1)S(1)}, u32[]{:S(2)}, u32[]{:S(2)}) async-start(bf16[32,32,512]{2,1,0:T(8,128)(2,1)} %look.1), calls=%async_computation.1 | async-start | bytes 2097152 | tf_op jit(solution)/shard_map/all_to_all | solution.py:310
  74.6 2.1 %collective-permute-start.5 = (bf16[64,4096]{1,0:T(8,128)(2,1)S(1)}, bf16[64,4096]{1,0:T(8,128)(2,1)S(1)}, u32[]{:S(2)}, u32[]{:S(2)}) collective-permute-start(bf16[64,4096]{1,0:T(8,128)(2,1)S(1)} %pad_maximum_fusion), channel_id=1, source_target_pairs={{0,4},{1,5},{2,6},{3,7},{4,0},{5,1},{6,2},{7,3},{8,12},{9,13},{10,... | collective-permute-start | bytes 1572872 | tf_op jit(solution)/shard_map/ppermute | solution.py:274
  78.6 26.9 %collective-permute-done.3 = bf16[64,4096]{1,0:T(8,128)(2,1)S(1)} collective-permute-done((bf16[64,4096]{1,0:T(8,128)(2,1)S(1)}, bf16[64,4096]{1,0:T(8,128)(2,1)S(1)}, u32[]{:S(2)}, u32[]{:S(2)}) %collective-permute-start.3) | collective-permute-done | bytes 524320 | tf_op jit(solution)/shard_map/ppermute | solution.py:274
  107.2 12.6 %collective-permute-done.5 = bf16[64,4096]{1,0:T(8,128)(2,1)S(1)} collective-permute-done((bf16[64,4096]{1,0:T(8,128)(2,1)S(1)}, bf16[64,4096]{1,0:T(8,128)(2,1)S(1)}, u32[]{:S(2)}, u32[]{:S(2)}) %collective-permute-start.5) | collective-permute-done | bytes 524320 | tf_op jit(solution)/shard_map/ppermute | solution.py:274
  123.8 2.3 %all-to-all-done.1.e_ref = bf16[32,32,512]{2,1,0:T(8,128)(2,1)S(1)} async-done(((bf16[32,32,512]{2,1,0:T(8,128)(2,1)}), bf16[32,32,512]{2,1,0:T(8,128)(2,1)S(1)}, u32[]{:S(2)}, u32[]{:S(2)}) %all-to-all-start.1) | async-done | bytes 1048608 | tf_op jit(solution)/shard_map/all_to_all | solution.py:310
  127.0 4.3 %all-to-all-start.2 = ((f32[8,2,512]{2,1,0:T(2,128)}), f32[8,2,512]{2,1,0:T(2,128)S(1)}, u32[]{:S(2)}, u32[]{:S(2)}) async-start(f32[8,2,512]{2,1,0:T(2,128)} %broadcast_in_dim.77), calls=%async_computation.2 | async-start | bytes 65536 | tf_op jit(solution)/shard_map/all_to_all | solution.py:328
  131.3 5.4 %prep.1.refs_0_ = bf16[512,1792]{1,0:T(8,128)(2,1)S(1)} custom-call(bf16[512,896]{1,0:T(8,128)(2,1)S(1)} %copy-done.3, bf16[32,32,512]{2,1,0:T(8,128)(2,1)S(1)} %all-to-all-done.1.e_ref, s32[1,1792]{1,0:T(1,128)S(1)} %broadcast_in_dim.72.s_ref), custom_call_target="tpu_custom_call" | custom-call | flops 3523215360 | bytes 8388608 | tf_op jit(solution)/shard_map/prep/pallas_call | solution.py:112
  138.0 14.0 %mix_sent.1 = (bf16[4,512,256]{2,1,0:T(8,128)(2,1)}, bf16[2,512,256]{2,1,0:T(8,128)(2,1)}, bf16[2,512,256]{2,1,0:T(8,128)(2,1)S(1)}, bf16[2,512,256]{2,1,0:T(8,128)(2,1)}, bf16[512,1792]{1,0:T(8,128)(2,1)}) custom-call(s32[10]{0:T(128)S(1)} %stack.179.order_ref, bf16[512,1792]{1,0:T(8,128)(2,1)} %copy-done.4, f32[1,1792]{1,0:T(1,128)S(1)} %broadcast_in_dim.76.refs_1_, ...), custom_call_target="tpu_custom_call" | custom-call | flops 4697620480 | bytes 18350080 | tf_op jit(solution)/shard_map/mix_sent/pallas_call | solution.py:187
  152.0 2.1 %collective-permute-start.7 = (bf16[4,512,256]{2,1,0:T(8,128)(2,1)}, bf16[4,512,256]{2,1,0:T(8,128)(2,1)S(1)}, u32[]{:S(2)}, u32[]{:S(2)}) collective-permute-start(bf16[4,512,256]{2,1,0:T(8,128)(2,1)} %get-tuple-element.20), channel_id=1, source_target_pairs={{0,128},{32,160},{64,192},{96,224},{128,0},{160,32},{192,64},{224,... | collective-permute-start | bytes 3145736 | tf_op jit(solution)/shard_map/ppermute | solution.py:236
  154.1 2.7 %collective-permute-start.10 = (bf16[2,512,256]{2,1,0:T(8,128)(2,1)}, bf16[2,512,256]{2,1,0:T(8,128)(2,1)S(1)}, u32[]{:S(2)}, u32[]{:S(2)}) collective-permute-start(bf16[2,512,256]{2,1,0:T(8,128)(2,1)} %get-tuple-element.24), channel_id=1, source_target_pairs={{0,96},{32,0},{64,32},{96,64},{128,224},{160,128},{192,160},{224,1... | collective-permute-start | bytes 1572872 | tf_op jit(solution)/shard_map/ppermute | solution.py:236
  156.8 2.3 %collective-permute-start.9 = (bf16[2,512,256]{2,1,0:T(8,128)(2,1)S(1)}, bf16[2,512,256]{2,1,0:T(8,128)(2,1)S(1)}, u32[]{:S(2)}, u32[]{:S(2)}) collective-permute-start(bf16[2,512,256]{2,1,0:T(8,128)(2,1)S(1)} %get-tuple-element.23), channel_id=1, source_target_pairs={{0,64},{32,96},{64,0},{96,32},{128,192},{160,224},{192,128},{224,1... | collective-permute-start | bytes 1572872 | tf_op jit(solution)/shard_map/ppermute | solution.py:236
  160.7 8.1 %mix_kept.1 = (f32[4,512,256]{2,1,0:T(8,128)}, f32[2,512,256]{2,1,0:T(8,128)S(1)}) custom-call(s32[6]{0:T(128)S(1)} %stack.168.order_ref, bf16[512,1792]{1,0:T(8,128)(2,1)S(1)} %copy-done.2, bf16[1280,4096]{1,0:T(8,128)(2,1)} %all-gather.2.cloned.1.call-done.refs_4_.refs_0_, bf16[256,4096]{1,0:T(8,128)(2,1)} %constant_dynamic-update-slice_fusion.refs_5_.refs_1_, ...), custom_call_target="tpu_custom_call" | custom-call | flops 2818572288 | bytes 11010048 | tf_op jit(solution)/shard_map/mix_kept/pallas_call | solution.py:200
  168.8 10.2 %collective-permute-done.10.b_3 = bf16[2,512,256]{2,1,0:T(8,128)(2,1)S(1)} collective-permute-done((bf16[2,512,256]{2,1,0:T(8,128)(2,1)}, bf16[2,512,256]{2,1,0:T(8,128)(2,1)S(1)}, u32[]{:S(2)}, u32[]{:S(2)}) %collective-permute-start.10) | collective-permute-done | bytes 524320 | tf_op jit(solution)/shard_map/ppermute | solution.py:236
  178.9 3.3 %collective-permute-done.8.b_1 = bf16[2,512,256]{2,1,0:T(8,128)(2,1)S(1)} collective-permute-done((bf16[2,512,256]{2,1,0:T(8,128)(2,1)}, bf16[2,512,256]{2,1,0:T(8,128)(2,1)S(1)}, u32[]{:S(2)}, u32[]{:S(2)}) %collective-permute-start.8) | collective-permute-done | bytes 524320 | tf_op jit(solution)/shard_map/ppermute | solution.py:236
  188.6 8.4 %collective-permute-done.11.a_1 = bf16[512,256]{1,0:T(8,128)(2,1)S(1)} collective-permute-done((bf16[512,256]{1,0:T(8,128)(2,1)S(1)}, bf16[512,256]{1,0:T(8,128)(2,1)S(1)}, u32[]{:S(2)}, u32[]{:S(2)}) %collective-permute-start.11) | collective-permute-done | bytes 262176 | tf_op jit(solution)/shard_map/ppermute | solution.py:236
  (86 shorter events, 26.9 us)
Async XLA Ops:
  6.5 131.5 %all-gather.2.cloned.1.call-start = ((), (), s32[]{:S(2)}) async-start(), calls=%async_computation.3 | async-start | bytes 10813440 | tf_op jit(solution)/shard_map/all_gather | solution.py:304
  10.0 62.4 %collective-permute-start = (bf16[16,4096]{1,0:T(8,128)(2,1)S(1)}, bf16[16,4096]{1,0:T(8,128)(2,1)S(1)}, u32[]{:S(2)}, u32[]{:S(2)}) collective-permute-start(bf16[16,4096]{1,0:T(8,128)(2,1)S(1)} %get-tuple-element.33), channel_id=1, source_target_pairs={{0,8},{1,9},{2,10},{3,11},{4,12},{5,13},{6,14},{7,15},{8,16},{9,17... | collective-permute-start | bytes 393224 | tf_op jit(solution)/shard_map/ppermute | solution.py:274
  13.3 59.1 %collective-permute-start.1 = (bf16[16,4096]{1,0:T(8,128)(2,1)S(1)}, bf16[16,4096]{1,0:T(8,128)(2,1)S(1)}, u32[]{:S(2)}, u32[]{:S(2)}) collective-permute-start(bf16[16,4096]{1,0:T(8,128)(2,1)S(1)} %get-tuple-element.33), channel_id=1, source_target_pairs={{0,24},{1,25},{2,26},{3,27},{4,28},{5,29},{6,30},{7,31},{8,0},{9,1... | collective-permute-start | bytes 393224 | tf_op jit(solution)/shard_map/ppermute | solution.py:274
  16.3 56.1 %collective-permute-start.2 = (bf16[16,4096]{1,0:T(8,128)(2,1)S(1)}, bf16[16,4096]{1,0:T(8,128)(2,1)S(1)}, u32[]{:S(2)}, u32[]{:S(2)}) collective-permute-start(bf16[16,4096]{1,0:T(8,128)(2,1)S(1)} %get-tuple-element.33), channel_id=1, source_target_pairs={{0,16},{1,17},{2,18},{3,19},{4,20},{5,21},{6,22},{7,23},{8,24},{9,... | collective-permute-start | bytes 393224 | tf_op jit(solution)/shard_map/ppermute | solution.py:274
  22.6 16.1 %all-to-all-start = ((s32[32,1,512]{2,1,0:T(1,128)}), s32[32,1,512]{2,1,0:T(1,128)S(1)}, u32[]{:S(2)}, u32[]{:S(2)}) async-start(s32[32,1,512]{2,1,0:T(1,128)} %broadcast_in_dim.67), calls=%async_computation | async-start | bytes 131072 | tf_op jit(solution)/shard_map/all_to_all | solution.py:301
  40.3 3.4 %copy-start = (f32[16384,128]{1,0:T(8,128)S(1)}, f32[16384,128]{1,0:T(8,128)}, u32[]{:S(2)}) copy-start(f32[16384,128]{1,0:T(8,128)} %turn.1) | copy-start | bytes 25165828
  65.4 60.7 %all-to-all-start.1 = ((bf16[32,32,512]{2,1,0:T(8,128)(2,1)}), bf16[32,32,512]{2,1,0:T(8,128)(2,1)S(1)}, u32[]{:S(2)}, u32[]{:S(2)}) async-start(bf16[32,32,512]{2,1,0:T(8,128)(2,1)} %look.1), calls=%async_computation.1 | async-start | bytes 2097152 | tf_op jit(solution)/shard_map/all_to_all | solution.py:310
  72.5 33.1 %collective-permute-start.3 = (bf16[64,4096]{1,0:T(8,128)(2,1)S(1)}, bf16[64,4096]{1,0:T(8,128)(2,1)S(1)}, u32[]{:S(2)}, u32[]{:S(2)}) collective-permute-start(bf16[64,4096]{1,0:T(8,128)(2,1)S(1)} %pad_maximum_fusion), channel_id=1, source_target_pairs={{0,2},{1,3},{2,4},{3,5},{4,6},{5,7},{6,0},{7,1},{8,10},{9,11},{10,... | collective-permute-start | bytes 1572872 | tf_op jit(solution)/shard_map/ppermute | solution.py:274
  74.0 32.4 %collective-permute-start.4 = (bf16[64,4096]{1,0:T(8,128)(2,1)S(1)}, bf16[64,4096]{1,0:T(8,128)(2,1)S(1)}, u32[]{:S(2)}, u32[]{:S(2)}) collective-permute-start(bf16[64,4096]{1,0:T(8,128)(2,1)S(1)} %pad_maximum_fusion), channel_id=1, source_target_pairs={{0,6},{1,7},{2,0},{3,1},{4,2},{5,3},{6,4},{7,5},{8,14},{9,15},{10,... | collective-permute-start | bytes 1572872 | tf_op jit(solution)/shard_map/ppermute | solution.py:274
  74.6 45.2 %collective-permute-start.5 = (bf16[64,4096]{1,0:T(8,128)(2,1)S(1)}, bf16[64,4096]{1,0:T(8,128)(2,1)S(1)}, u32[]{:S(2)}, u32[]{:S(2)}) collective-permute-start(bf16[64,4096]{1,0:T(8,128)(2,1)S(1)} %pad_maximum_fusion), channel_id=1, source_target_pairs={{0,4},{1,5},{2,6},{3,7},{4,0},{5,1},{6,2},{7,3},{8,12},{9,13},{10,... | collective-permute-start | bytes 1572872 | tf_op jit(solution)/shard_map/ppermute | solution.py:274
  77.3 46.2 %copy-start.3 = (bf16[512,896]{1,0:T(8,128)(2,1)S(1)}, bf16[512,896]{1,0:T(8,128)(2,1)}, u32[]{:S(2)}) copy-start(bf16[512,896]{1,0:T(8,128)(2,1)} %h_ref.1) | copy-start | bytes 2752516
  120.6 17.4 %collective-permute-start.6 = (bf16[256,4096]{1,0:T(8,128)(2,1)}, bf16[256,4096]{1,0:T(8,128)(2,1)}, u32[]{:S(2)}, u32[]{:S(2)}) collective-permute-start(bf16[256,4096]{1,0:T(8,128)(2,1)} %constant_dynamic-update-slice_fusion.refs_5_.refs_1_), channel_id=1, source_target_pairs={{0,1},{1,0},{2,3},{3,2},{4,5},{5,4},{6,7},{7,6},{8,9},{9,8},{10,11... | collective-permute-start | bytes 6291464 | tf_op jit(solution)/shard_map/ppermute | solution.py:274
  127.0 10.9 %all-to-all-start.2 = ((f32[8,2,512]{2,1,0:T(2,128)}), f32[8,2,512]{2,1,0:T(2,128)S(1)}, u32[]{:S(2)}, u32[]{:S(2)}) async-start(f32[8,2,512]{2,1,0:T(2,128)} %broadcast_in_dim.77), calls=%async_computation.2 | async-start | bytes 65536 | tf_op jit(solution)/shard_map/all_to_all | solution.py:328
  136.7 1.2 copy-start.4
  152.0 30.2 %collective-permute-start.7 = (bf16[4,512,256]{2,1,0:T(8,128)(2,1)}, bf16[4,512,256]{2,1,0:T(8,128)(2,1)S(1)}, u32[]{:S(2)}, u32[]{:S(2)}) collective-permute-start(bf16[4,512,256]{2,1,0:T(8,128)(2,1)} %get-tuple-element.20), channel_id=1, source_target_pairs={{0,128},{32,160},{64,192},{96,224},{128,0},{160,32},{192,64},{224,... | collective-permute-start | bytes 3145736 | tf_op jit(solution)/shard_map/ppermute | solution.py:236
  154.1 24.8 %collective-permute-start.10 = (bf16[2,512,256]{2,1,0:T(8,128)(2,1)}, bf16[2,512,256]{2,1,0:T(8,128)(2,1)S(1)}, u32[]{:S(2)}, u32[]{:S(2)}) collective-permute-start(bf16[2,512,256]{2,1,0:T(8,128)(2,1)} %get-tuple-element.24), channel_id=1, source_target_pairs={{0,96},{32,0},{64,32},{96,64},{128,224},{160,128},{192,160},{224,1... | collective-permute-start | bytes 1572872 | tf_op jit(solution)/shard_map/ppermute | solution.py:236
  156.8 25.4 %collective-permute-start.8 = (bf16[2,512,256]{2,1,0:T(8,128)(2,1)}, bf16[2,512,256]{2,1,0:T(8,128)(2,1)S(1)}, u32[]{:S(2)}, u32[]{:S(2)}) collective-permute-start(bf16[2,512,256]{2,1,0:T(8,128)(2,1)} %get-tuple-element.22), channel_id=1, source_target_pairs={{0,32},{32,64},{64,96},{96,0},{128,160},{160,192},{192,224},{224,1... | collective-permute-start | bytes 1572872 | tf_op jit(solution)/shard_map/ppermute | solution.py:236
  156.8 25.4 %collective-permute-start.9 = (bf16[2,512,256]{2,1,0:T(8,128)(2,1)S(1)}, bf16[2,512,256]{2,1,0:T(8,128)(2,1)S(1)}, u32[]{:S(2)}, u32[]{:S(2)}) collective-permute-start(bf16[2,512,256]{2,1,0:T(8,128)(2,1)S(1)} %get-tuple-element.23), channel_id=1, source_target_pairs={{0,64},{32,96},{64,0},{96,32},{128,192},{160,224},{192,128},{224,1... | collective-permute-start | bytes 1572872 | tf_op jit(solution)/shard_map/ppermute | solution.py:236
  159.2 1.5 copy-start.2
  182.2 1.6 copy-start.1
  184.7 12.2 %collective-permute-start.11 = (bf16[512,256]{1,0:T(8,128)(2,1)S(1)}, bf16[512,256]{1,0:T(8,128)(2,1)S(1)}, u32[]{:S(2)}, u32[]{:S(2)}) collective-permute-start(bf16[512,256]{1,0:T(8,128)(2,1)S(1)} %get-tuple-element.26), channel_id=1, source_target_pairs={{0,32},{32,64},{64,96},{96,0},{128,160},{160,192},{192,224},{224,1... | collective-permute-start | bytes 786440 | tf_op jit(solution)/shard_map/ppermute | solution.py:236
  184.8 12.2 %collective-permute-start.12 = (bf16[512,256]{1,0:T(8,128)(2,1)S(1)}, bf16[512,256]{1,0:T(8,128)(2,1)S(1)}, u32[]{:S(2)}, u32[]{:S(2)}) collective-permute-start(bf16[512,256]{1,0:T(8,128)(2,1)S(1)} %get-tuple-element.27), channel_id=1, source_target_pairs={{0,64},{32,96},{64,0},{96,32},{128,192},{160,224},{192,128},{224,1... | collective-permute-start | bytes 786440 | tf_op jit(solution)/shard_map/ppermute | solution.py:236
  186.5 11.1 %collective-permute-start.13 = (bf16[512,256]{1,0:T(8,128)(2,1)S(1)}, bf16[512,256]{1,0:T(8,128)(2,1)S(1)}, u32[]{:S(2)}, u32[]{:S(2)}) collective-permute-start(bf16[512,256]{1,0:T(8,128)(2,1)S(1)} %get-tuple-element.28), channel_id=1, source_target_pairs={{0,96},{32,0},{64,32},{96,64},{128,224},{160,128},{192,160},{224,1... | collective-permute-start | bytes 786440 | tf_op jit(solution)/shard_map/ppermute | solution.py:236
  188.0 9.6 %collective-permute-start.14 = (bf16[512,256]{1,0:T(8,128)(2,1)S(1)}, bf16[512,256]{1,0:T(8,128)(2,1)S(1)}, u32[]{:S(2)}, u32[]{:S(2)}) collective-permute-start(bf16[512,256]{1,0:T(8,128)(2,1)S(1)} %get-tuple-element.30), channel_id=1, source_target_pairs={{0,128},{32,160},{64,192},{96,224},{128,0},{160,32},{192,64},{224,... | collective-permute-start | bytes 786440 | tf_op jit(solution)/shard_map/ppermute | solution.py:236
Sparse Core Ops, SparseCore 0:
  9.9 108.5 all-gather.1

commit v5 on v4

--- a/solution.py
+++ b/solution.py
@@ -246,7 +246,7 @@
         grid=(tokens // step,),
         in_specs=[deep(4), deep(4), deep(2), deep(2), deep(2), deep(2)],
         out_specs=[flat] * 6,
-        compiler_params=pltpu.CompilerParams(vmem_limit_bytes=16 << 20),
+        compiler_params=pltpu.CompilerParams(vmem_limit_bytes=58 << 20),
         name="fold",
     )(a_keep, a_in, b_keep, *b_in)
     a_more = [to(a, 0, d) for a, d in ((a_1, 1), (a_2, 2), (a_3, 3))]

time: 207 us -> 211 us (1.019)
  Pallas kernels: 58.7 us -> 61.7 us
    pallas_call x1, Pallas kernels: 0.88 us -> 4.43 us  [fold(): pl.pallas_call(fold_kernel, out_shape=[shape(bf)] * 3 + [shape(f32), shap...]
    unnamed x15 -> x19, local copies, waits for them, and re-layouts: 11.4 us -> 13 us
  transfers between devices with their start and end apart: 19 -> 19, of which waited for: 8 -> 9; matrix products, arithmetic and copies ran while one was open for 7% -> 7% of each run, Pallas kernels for 21% -> 20%
where the time goes in v5:
time: 211 us; the launch traced here: 209 us
  waiting for transfers between devices  66.1 us (31%)
  Pallas kernels  61.7 us (29%)
  starting transfers between devices  43 us (20%)
  local copies, waits for them, and re-layouts  20.7 us (10%)
  between operations  13.9 us (7%)
  other arithmetic  4.06 us (2%)
    ppermute x7, waiting for transfers between devices, to(): return lax.ppermute(a, 'fsdp', pairs)  39.5 us
    pallas_call x1, Pallas kernels, look(): pl.pallas_call(functools.partial(look_kernel, quarter), out_shape=jax.Sha...  21.6 us
    ppermute x8, waiting for transfers between devices, to(): return lax.ppermute(a, 'section', pairs)  21.6 us
    ppermute x7, starting transfers between devices, to(): return lax.ppermute(a, 'fsdp', pairs)  15.5 us
    pallas_call x1, Pallas kernels, mix(): pl.pallas_call(functools.partial(send_kernel, len(pieces)), out_shape=[sh...  13.5 us
    unnamed x19, local copies, waits for them, and re-layouts  13 us
    ppermute x8, starting transfers between devices, to(): return lax.ppermute(a, 'section', pairs)  10.9 us
    pallas_call x1, Pallas kernels, mix(): pl.pallas_call(functools.partial(keep_kernel, len(pieces)), out_shape=[sh...  8.06 us
  transfers between devices with their start and end apart: 19, of which 9 were waited for; matrix products, arithmetic and copies ran while one was open for 7% of the time, Pallas kernels for 20%

profile of v5, /device:TPU:2, one launch (start us, length us, event | category | flops | bytes accessed | tf_op | source)
XLA Modules:
  0.0 209.5 jit_solution(2166583737824570737)
XLA Ops:
  10.0 3.3 %collective-permute-start = (bf16[16,4096]{1,0:T(8,128)(2,1)S(1)}, bf16[16,4096]{1,0:T(8,128)(2,1)S(1)}, u32[]{:S(2)}, u32[]{:S(2)}) collective-permute-start(bf16[16,4096]{1,0:T(8,128)(2,1)S(1)} %get-tuple-element.33), channel_id=1, source_target_pairs={{0,8},{1,9},{2,10},{3,11},{4,12},{5,13},{6,14},{7,15},{8,16},{9,17... | collective-permute-start | bytes 393224 | tf_op jit(solution)/shard_map/ppermute | solution.py:274
  13.2 3.0 %collective-permute-start.1 = (bf16[16,4096]{1,0:T(8,128)(2,1)S(1)}, bf16[16,4096]{1,0:T(8,128)(2,1)S(1)}, u32[]{:S(2)}, u32[]{:S(2)}) collective-permute-start(bf16[16,4096]{1,0:T(8,128)(2,1)S(1)} %get-tuple-element.33), channel_id=1, source_target_pairs={{0,24},{1,25},{2,26},{3,27},{4,28},{5,29},{6,30},{7,31},{8,0},{9,1... | collective-permute-start | bytes 393224 | tf_op jit(solution)/shard_map/ppermute | solution.py:274
  16.3 5.0 %collective-permute-start.2 = (bf16[16,4096]{1,0:T(8,128)(2,1)S(1)}, bf16[16,4096]{1,0:T(8,128)(2,1)S(1)}, u32[]{:S(2)}, u32[]{:S(2)}) collective-permute-start(bf16[16,4096]{1,0:T(8,128)(2,1)S(1)} %get-tuple-element.33), channel_id=1, source_target_pairs={{0,16},{1,17},{2,18},{3,19},{4,20},{5,21},{6,22},{7,23},{8,24},{9,... | collective-permute-start | bytes 393224 | tf_op jit(solution)/shard_map/ppermute | solution.py:274
  22.6 5.3 %all-to-all-start = ((s32[32,1,512]{2,1,0:T(1,128)}), s32[32,1,512]{2,1,0:T(1,128)S(1)}, u32[]{:S(2)}, u32[]{:S(2)}) async-start(s32[32,1,512]{2,1,0:T(1,128)} %broadcast_in_dim.67), calls=%async_computation | async-start | bytes 131072 | tf_op jit(solution)/shard_map/all_to_all | solution.py:301
  28.7 7.3 %turn.1 = f32[16384,128]{1,0:T(8,128)} custom-call(bf16[28,65536]{1,0:T(8,128)(2,1)} %refs_3_.1, bf16[28,65536]{1,0:T(8,128)(2,1)} %refs_3_.1, bf16[28,65536]{1,0:T(8,128)(2,1)} %refs_3_.1, bf16[28,65536]{1,0:T(8,128)(2,1)} %refs_3_.1), custom_call_target="tpu_custom_call" | custom-call | tf_op jit(solution)/shard_map/turn/pallas_call | solution.py:39
  36.0 2.8 %all-to-all-done = s32[32,1,512]{2,1,0:T(1,128)S(1)} async-done(((s32[32,1,512]{2,1,0:T(1,128)}), s32[32,1,512]{2,1,0:T(1,128)S(1)}, u32[]{:S(2)}, u32[]{:S(2)}) %all-to-all-start) | async-done | bytes 65568 | tf_op jit(solution)/shard_map/all_to_all | solution.py:301
  40.5 3.4 %copy-done = f32[16384,128]{1,0:T(8,128)S(1)} copy-done((f32[16384,128]{1,0:T(8,128)S(1)}, f32[16384,128]{1,0:T(8,128)}, u32[]{:S(2)}) %copy-start) | copy-done | bytes 8388632
  43.9 21.6 %look.1 = bf16[32,32,512]{2,1,0:T(8,128)(2,1)} custom-call(s32[32,1,512]{2,1,0:T(1,128)S(1)} %and_select_fusion.1.row_ref, s32[32,1,512]{2,1,0:T(1,128)S(1)} %get-tuple-element.31.grp_ref, f32[16384,1,128]{2,1,0:T(1,128)S(1)} %bitcast.61), custom_call_target="tpu_custom_call" | custom-call | tf_op jit(solution)/shard_map/look/pallas_call | solution.py:73
  65.5 7.0 %all-to-all-start.1 = ((bf16[32,32,512]{2,1,0:T(8,128)(2,1)}), bf16[32,32,512]{2,1,0:T(8,128)(2,1)S(1)}, u32[]{:S(2)}, u32[]{:S(2)}) async-start(bf16[32,32,512]{2,1,0:T(8,128)(2,1)} %look.1), calls=%async_computation.1 | async-start | bytes 2097152 | tf_op jit(solution)/shard_map/all_to_all | solution.py:310
  74.7 2.1 collective-permute-start.5
  78.7 26.0 %collective-permute-done.3 = bf16[64,4096]{1,0:T(8,128)(2,1)S(1)} collective-permute-done((bf16[64,4096]{1,0:T(8,128)(2,1)S(1)}, bf16[64,4096]{1,0:T(8,128)(2,1)S(1)}, u32[]{:S(2)}, u32[]{:S(2)}) %collective-permute-start.3) | collective-permute-done | bytes 524320 | tf_op jit(solution)/shard_map/ppermute | solution.py:274
  106.7 13.1 %collective-permute-done.5 = bf16[64,4096]{1,0:T(8,128)(2,1)S(1)} collective-permute-done((bf16[64,4096]{1,0:T(8,128)(2,1)S(1)}, bf16[64,4096]{1,0:T(8,128)(2,1)S(1)}, u32[]{:S(2)}, u32[]{:S(2)}) %collective-permute-start.5) | collective-permute-done | bytes 524320 | tf_op jit(solution)/shard_map/ppermute | solution.py:274
  123.9 2.2 %all-to-all-done.1.e_ref = bf16[32,32,512]{2,1,0:T(8,128)(2,1)S(1)} async-done(((bf16[32,32,512]{2,1,0:T(8,128)(2,1)}), bf16[32,32,512]{2,1,0:T(8,128)(2,1)S(1)}, u32[]{:S(2)}, u32[]{:S(2)}) %all-to-all-start.1) | async-done | bytes 1048608 | tf_op jit(solution)/shard_map/all_to_all | solution.py:310
  127.0 4.3 %all-to-all-start.2 = ((f32[8,2,512]{2,1,0:T(2,128)}), f32[8,2,512]{2,1,0:T(2,128)S(1)}, u32[]{:S(2)}, u32[]{:S(2)}) async-start(f32[8,2,512]{2,1,0:T(2,128)} %broadcast_in_dim.77), calls=%async_computation.2 | async-start | bytes 65536 | tf_op jit(solution)/shard_map/all_to_all | solution.py:328
  131.3 5.4 %prep.1.refs_0_ = bf16[512,1792]{1,0:T(8,128)(2,1)S(1)} custom-call(bf16[512,896]{1,0:T(8,128)(2,1)S(1)} %copy-done.3, bf16[32,32,512]{2,1,0:T(8,128)(2,1)S(1)} %all-to-all-done.1.e_ref, s32[1,1792]{1,0:T(1,128)S(1)} %broadcast_in_dim.72.s_ref), custom_call_target="tpu_custom_call" | custom-call | flops 3523215360 | bytes 8388608 | tf_op jit(solution)/shard_map/prep/pallas_call | solution.py:112
  138.0 13.5 %mix_sent.1 = (bf16[4,512,256]{2,1,0:T(8,128)(2,1)S(1)}, bf16[2,512,256]{2,1,0:T(8,128)(2,1)S(1)}, bf16[2,512,256]{2,1,0:T(8,128)(2,1)S(1)}, bf16[2,512,256]{2,1,0:T(8,128)(2,1)S(1)}, bf16[512,1792]{1,0:T(8,128)(2,1)}) custom-call(s32[10]{0:T(128)S(1)} %stack.179.order_ref, bf16[512,1792]{1,0:T(8,128)(2,1)} %copy-done.6, ...), custom_call_target="tpu_custom_call" | custom-call | flops 4697620480 | bytes 18350080 | tf_op jit(solution)/shard_map/mix_sent/pallas_call | solution.py:187
  151.5 2.0 collective-permute-start.7
  153.6 2.7 %collective-permute-start.10 = (bf16[2,512,256]{2,1,0:T(8,128)(2,1)S(1)}, bf16[2,512,256]{2,1,0:T(8,128)(2,1)}, u32[]{:S(2)}, u32[]{:S(2)}) collective-permute-start(bf16[2,512,256]{2,1,0:T(8,128)(2,1)S(1)} %get-tuple-element.24), channel_id=1, source_target_pairs={{0,96},{32,0},{64,32},{96,64},{128,224},{160,128},{192,160},{224,1... | collective-permute-start | bytes 1572872 | tf_op jit(solution)/shard_map/ppermute | solution.py:236
  156.2 2.3 %collective-permute-start.9 = (bf16[2,512,256]{2,1,0:T(8,128)(2,1)S(1)}, bf16[2,512,256]{2,1,0:T(8,128)(2,1)}, u32[]{:S(2)}, u32[]{:S(2)}) collective-permute-start(bf16[2,512,256]{2,1,0:T(8,128)(2,1)S(1)} %get-tuple-element.23), channel_id=1, source_target_pairs={{0,64},{32,96},{64,0},{96,32},{128,192},{160,224},{192,128},{224,1... | collective-permute-start | bytes 1572872 | tf_op jit(solution)/shard_map/ppermute | solution.py:236
  160.2 8.1 %mix_kept.1 = (f32[4,512,256]{2,1,0:T(8,128)}, f32[2,512,256]{2,1,0:T(8,128)S(1)}) custom-call(s32[6]{0:T(128)S(1)} %stack.168.order_ref, bf16[512,1792]{1,0:T(8,128)(2,1)S(1)} %copy-done.1, bf16[1280,4096]{1,0:T(8,128)(2,1)} %all-gather.2.cloned.1.call-done.refs_4_.refs_0_, bf16[256,4096]{1,0:T(8,128)(2,1)} %constant_dynamic-update-slice_fusion.refs_5_.refs_1_, ...), custom_call_target="tpu_custom_call" | custom-call | flops 2818572288 | bytes 11010048 | tf_op jit(solution)/shard_map/mix_kept/pallas_call | solution.py:200
  169.2 8.8 %collective-permute-done.10.b_3 = bf16[2,512,256]{2,1,0:T(8,128)(2,1)} collective-permute-done((bf16[2,512,256]{2,1,0:T(8,128)(2,1)S(1)}, bf16[2,512,256]{2,1,0:T(8,128)(2,1)}, u32[]{:S(2)}, u32[]{:S(2)}) %collective-permute-start.10) | collective-permute-done | bytes 524320 | tf_op jit(solution)/shard_map/ppermute | solution.py:236
  178.1 3.5 %collective-permute-done.8.b_1 = bf16[2,512,256]{2,1,0:T(8,128)(2,1)} collective-permute-done((bf16[2,512,256]{2,1,0:T(8,128)(2,1)S(1)}, bf16[2,512,256]{2,1,0:T(8,128)(2,1)}, u32[]{:S(2)}, u32[]{:S(2)}) %collective-permute-start.8) | collective-permute-done | bytes 524320 | tf_op jit(solution)/shard_map/ppermute | solution.py:236
  181.6 4.4 %fold.1 = (bf16[512,256]{1,0:T(8,128)(2,1)}, bf16[512,256]{1,0:T(8,128)(2,1)}, bf16[512,256]{1,0:T(8,128)(2,1)}, f32[512,256]{1,0:T(8,128)}, bf16[512,256]{1,0:T(8,128)(2,1)}, /*index=5*/f32[512,256]{1,0:T(8,128)}) custom-call(f32[4,512,256]{2,1,0:T(8,128)} %get-tuple-element.19.a_keep, bf16[4,512,256]{2,1,0:T(8,128)(2,1)} %collective-permute-done.7.a_in, ...), custom_call_target="tpu_custom_call" | custom-call | tf_op jit(solution)/shard_map/fold/pallas_call | solution.py:243
  189.9 8.6 %collective-permute-done.11.a_1 = bf16[512,256]{1,0:T(8,128)(2,1)S(1)} collective-permute-done((bf16[512,256]{1,0:T(8,128)(2,1)}, bf16[512,256]{1,0:T(8,128)(2,1)S(1)}, u32[]{:S(2)}, u32[]{:S(2)}) %collective-permute-start.11) | collective-permute-done | bytes 262176 | tf_op jit(solution)/shard_map/ppermute | solution.py:236
  (90 shorter events, 29.8 us)
Async XLA Ops:
  6.5 131.5 %all-gather.2.cloned.1.call-start = ((), (), s32[]{:S(2)}) async-start(), calls=%async_computation.3 | async-start | bytes 10813440 | tf_op jit(solution)/shard_map/all_gather | solution.py:304
  10.0 62.5 %collective-permute-start = (bf16[16,4096]{1,0:T(8,128)(2,1)S(1)}, bf16[16,4096]{1,0:T(8,128)(2,1)S(1)}, u32[]{:S(2)}, u32[]{:S(2)}) collective-permute-start(bf16[16,4096]{1,0:T(8,128)(2,1)S(1)} %get-tuple-element.33), channel_id=1, source_target_pairs={{0,8},{1,9},{2,10},{3,11},{4,12},{5,13},{6,14},{7,15},{8,16},{9,17... | collective-permute-start | bytes 393224 | tf_op jit(solution)/shard_map/ppermute | solution.py:274
  13.2 59.3 %collective-permute-start.1 = (bf16[16,4096]{1,0:T(8,128)(2,1)S(1)}, bf16[16,4096]{1,0:T(8,128)(2,1)S(1)}, u32[]{:S(2)}, u32[]{:S(2)}) collective-permute-start(bf16[16,4096]{1,0:T(8,128)(2,1)S(1)} %get-tuple-element.33), channel_id=1, source_target_pairs={{0,24},{1,25},{2,26},{3,27},{4,28},{5,29},{6,30},{7,31},{8,0},{9,1... | collective-permute-start | bytes 393224 | tf_op jit(solution)/shard_map/ppermute | solution.py:274
  16.3 56.2 %collective-permute-start.2 = (bf16[16,4096]{1,0:T(8,128)(2,1)S(1)}, bf16[16,4096]{1,0:T(8,128)(2,1)S(1)}, u32[]{:S(2)}, u32[]{:S(2)}) collective-permute-start(bf16[16,4096]{1,0:T(8,128)(2,1)S(1)} %get-tuple-element.33), channel_id=1, source_target_pairs={{0,16},{1,17},{2,18},{3,19},{4,20},{5,21},{6,22},{7,23},{8,24},{9,... | collective-permute-start | bytes 393224 | tf_op jit(solution)/shard_map/ppermute | solution.py:274
  22.6 16.1 %all-to-all-start = ((s32[32,1,512]{2,1,0:T(1,128)}), s32[32,1,512]{2,1,0:T(1,128)S(1)}, u32[]{:S(2)}, u32[]{:S(2)}) async-start(s32[32,1,512]{2,1,0:T(1,128)} %broadcast_in_dim.67), calls=%async_computation | async-start | bytes 131072 | tf_op jit(solution)/shard_map/all_to_all | solution.py:301
  40.5 3.4 %copy-start = (f32[16384,128]{1,0:T(8,128)S(1)}, f32[16384,128]{1,0:T(8,128)}, u32[]{:S(2)}) copy-start(f32[16384,128]{1,0:T(8,128)} %turn.1) | copy-start | bytes 25165828
  65.5 60.6 %all-to-all-start.1 = ((bf16[32,32,512]{2,1,0:T(8,128)(2,1)}), bf16[32,32,512]{2,1,0:T(8,128)(2,1)S(1)}, u32[]{:S(2)}, u32[]{:S(2)}) async-start(bf16[32,32,512]{2,1,0:T(8,128)(2,1)} %look.1), calls=%async_computation.1 | async-start | bytes 2097152 | tf_op jit(solution)/shard_map/all_to_all | solution.py:310
  72.6 32.2 %collective-permute-start.3 = (bf16[64,4096]{1,0:T(8,128)(2,1)S(1)}, bf16[64,4096]{1,0:T(8,128)(2,1)S(1)}, u32[]{:S(2)}, u32[]{:S(2)}) collective-permute-start(bf16[64,4096]{1,0:T(8,128)(2,1)S(1)} %pad_maximum_fusion), channel_id=1, source_target_pairs={{0,2},{1,3},{2,4},{3,5},{4,6},{5,7},{6,0},{7,1},{8,10},{9,11},{10,... | collective-permute-start | bytes 1572872 | tf_op jit(solution)/shard_map/ppermute | solution.py:274
  74.1 31.8 %collective-permute-start.4 = (bf16[64,4096]{1,0:T(8,128)(2,1)S(1)}, bf16[64,4096]{1,0:T(8,128)(2,1)S(1)}, u32[]{:S(2)}, u32[]{:S(2)}) collective-permute-start(bf16[64,4096]{1,0:T(8,128)(2,1)S(1)} %pad_maximum_fusion), channel_id=1, source_target_pairs={{0,6},{1,7},{2,0},{3,1},{4,2},{5,3},{6,4},{7,5},{8,14},{9,15},{10,... | collective-permute-start | bytes 1572872 | tf_op jit(solution)/shard_map/ppermute | solution.py:274
  74.7 45.2 %collective-permute-start.5 = (bf16[64,4096]{1,0:T(8,128)(2,1)S(1)}, bf16[64,4096]{1,0:T(8,128)(2,1)S(1)}, u32[]{:S(2)}, u32[]{:S(2)}) collective-permute-start(bf16[64,4096]{1,0:T(8,128)(2,1)S(1)} %pad_maximum_fusion), channel_id=1, source_target_pairs={{0,4},{1,5},{2,6},{3,7},{4,0},{5,1},{6,2},{7,3},{8,12},{9,13},{10,... | collective-permute-start | bytes 1572872 | tf_op jit(solution)/shard_map/ppermute | solution.py:274
  77.4 46.2 %copy-start.3 = (bf16[512,896]{1,0:T(8,128)(2,1)S(1)}, bf16[512,896]{1,0:T(8,128)(2,1)}, u32[]{:S(2)}) copy-start(bf16[512,896]{1,0:T(8,128)(2,1)} %h_ref.1) | copy-start | bytes 2752516
  120.7 17.3 %collective-permute-start.6 = (bf16[256,4096]{1,0:T(8,128)(2,1)}, bf16[256,4096]{1,0:T(8,128)(2,1)}, u32[]{:S(2)}, u32[]{:S(2)}) collective-permute-start(bf16[256,4096]{1,0:T(8,128)(2,1)} %constant_dynamic-update-slice_fusion.refs_5_.refs_1_), channel_id=1, source_target_pairs={{0,1},{1,0},{2,3},{3,2},{4,5},{5,4},{6,7},{7,6},{8,9},{9,8},{10,11... | collective-permute-start | bytes 6291464 | tf_op jit(solution)/shard_map/ppermute | solution.py:274
  127.0 10.9 %all-to-all-start.2 = ((f32[8,2,512]{2,1,0:T(2,128)}), f32[8,2,512]{2,1,0:T(2,128)S(1)}, u32[]{:S(2)}, u32[]{:S(2)}) async-start(f32[8,2,512]{2,1,0:T(2,128)} %broadcast_in_dim.77), calls=%async_computation.2 | async-start | bytes 65536 | tf_op jit(solution)/shard_map/all_to_all | solution.py:328
  136.7 1.3 copy-start.6
  151.5 30.0 %collective-permute-start.7 = (bf16[4,512,256]{2,1,0:T(8,128)(2,1)S(1)}, bf16[4,512,256]{2,1,0:T(8,128)(2,1)}, u32[]{:S(2)}, u32[]{:S(2)}) collective-permute-start(bf16[4,512,256]{2,1,0:T(8,128)(2,1)S(1)} %get-tuple-element.20), channel_id=1, source_target_pairs={{0,128},{32,160},{64,192},{96,224},{128,0},{160,32},{192,64},{224,... | collective-permute-start | bytes 3145736 | tf_op jit(solution)/shard_map/ppermute | solution.py:236
  153.6 24.5 %collective-permute-start.10 = (bf16[2,512,256]{2,1,0:T(8,128)(2,1)S(1)}, bf16[2,512,256]{2,1,0:T(8,128)(2,1)}, u32[]{:S(2)}, u32[]{:S(2)}) collective-permute-start(bf16[2,512,256]{2,1,0:T(8,128)(2,1)S(1)} %get-tuple-element.24), channel_id=1, source_target_pairs={{0,96},{32,0},{64,32},{96,64},{128,224},{160,128},{192,160},{224,1... | collective-permute-start | bytes 1572872 | tf_op jit(solution)/shard_map/ppermute | solution.py:236
  156.2 25.3 %collective-permute-start.8 = (bf16[2,512,256]{2,1,0:T(8,128)(2,1)S(1)}, bf16[2,512,256]{2,1,0:T(8,128)(2,1)}, u32[]{:S(2)}, u32[]{:S(2)}) collective-permute-start(bf16[2,512,256]{2,1,0:T(8,128)(2,1)S(1)} %get-tuple-element.22), channel_id=1, source_target_pairs={{0,32},{32,64},{64,96},{96,0},{128,160},{160,192},{192,224},{224,1... | collective-permute-start | bytes 1572872 | tf_op jit(solution)/shard_map/ppermute | solution.py:236
  156.2 25.3 %collective-permute-start.9 = (bf16[2,512,256]{2,1,0:T(8,128)(2,1)S(1)}, bf16[2,512,256]{2,1,0:T(8,128)(2,1)}, u32[]{:S(2)}, u32[]{:S(2)}) collective-permute-start(bf16[2,512,256]{2,1,0:T(8,128)(2,1)S(1)} %get-tuple-element.23), channel_id=1, source_target_pairs={{0,64},{32,96},{64,0},{96,32},{128,192},{160,224},{192,128},{224,1... | collective-permute-start | bytes 1572872 | tf_op jit(solution)/shard_map/ppermute | solution.py:236
  158.6 1.5 copy-start.1
  186.0 12.5 %collective-permute-start.11 = (bf16[512,256]{1,0:T(8,128)(2,1)}, bf16[512,256]{1,0:T(8,128)(2,1)S(1)}, u32[]{:S(2)}, u32[]{:S(2)}) collective-permute-start(bf16[512,256]{1,0:T(8,128)(2,1)} %get-tuple-element.26), channel_id=1, source_target_pairs={{0,32},{32,64},{64,96},{96,0},{128,160},{160,192},{192,224},{224,1... | collective-permute-start | bytes 786440 | tf_op jit(solution)/shard_map/ppermute | solution.py:236
  186.1 12.4 %collective-permute-start.12 = (bf16[512,256]{1,0:T(8,128)(2,1)}, bf16[512,256]{1,0:T(8,128)(2,1)S(1)}, u32[]{:S(2)}, u32[]{:S(2)}) collective-permute-start(bf16[512,256]{1,0:T(8,128)(2,1)} %get-tuple-element.27), channel_id=1, source_target_pairs={{0,64},{32,96},{64,0},{96,32},{128,192},{160,224},{192,128},{224,1... | collective-permute-start | bytes 786440 | tf_op jit(solution)/shard_map/ppermute | solution.py:236
  187.8 11.3 %collective-permute-start.13 = (bf16[512,256]{1,0:T(8,128)(2,1)}, bf16[512,256]{1,0:T(8,128)(2,1)S(1)}, u32[]{:S(2)}, u32[]{:S(2)}) collective-permute-start(bf16[512,256]{1,0:T(8,128)(2,1)} %get-tuple-element.28), channel_id=1, source_target_pairs={{0,96},{32,0},{64,32},{96,64},{128,224},{160,128},{192,160},{224,1... | collective-permute-start | bytes 786440 | tf_op jit(solution)/shard_map/ppermute | solution.py:236
  189.3 9.8 %collective-permute-start.14 = (bf16[512,256]{1,0:T(8,128)(2,1)}, bf16[512,256]{1,0:T(8,128)(2,1)S(1)}, u32[]{:S(2)}, u32[]{:S(2)}) collective-permute-start(bf16[512,256]{1,0:T(8,128)(2,1)} %get-tuple-element.30), channel_id=1, source_target_pairs={{0,128},{32,160},{64,192},{96,224},{128,0},{160,32},{192,64},{224,... | collective-permute-start | bytes 786440 | tf_op jit(solution)/shard_map/ppermute | solution.py:236
  199.1 1.0 copy-start.4
  (2 other events, 2.1 us)
Sparse Core Ops, SparseCore 0:
  9.9 107.6 all-gather.1
